TPU v7x, 256 devices: a whole 4x4x8 slice. The times are simulated.
256 devices in a mesh: grp: 8 (over z), dev: 32 (over y, x, core).
Axes of the slice: x: 4, y: 4, z: 8, core: 2. Of those that a mesh axis runs over, the one named last changes fastest.
Arguments:
- encodings: bfloat16 [32768, 1024], P(('grp', 'dev')), may hold values from -6 to 6
- label_weights: bfloat16 [131072, 1024], P(('grp', 'dev')), may hold values from -0.1875 to 0.1875
- label_count: int32 [1024], P(('grp', 'dev')), may hold values from 32 to 128
- matched: int32 [32768, 8], P(('grp', 'dev')), may hold values from 0 to 1023, all different within a row; in each aligned block of 128 rows (0 to 127, 128 to 255, ...) at most 2 rows name the same one
- positive: int32 [32768, 8], P(('grp', 'dev')), may hold values from 0 to 127
Outputs:
- enc_grad: bfloat16 [32768, 1024], P(('grp', 'dev'))
- query_loss: float32 [32768], P(('grp', 'dev'))
- label_weight_gradient: float32 [131072, 1024], P(('grp', 'dev'))
Inputs may be any that keep to these rules, and one draw needn't show every extreme that they name: The 8 ids of a query differ; among the 128 queries of one device no cluster is matched more than 2 times, and in every draw some cluster is matched exactly 2 times by one device's queries; every cluster is matched somewhere.
All inputs are finite; a program needn't handle non-finite values.
Results may differ from a plain program's by a relative error of at most 0.011.
Values may be sent and summed in bfloat16 or wider, within the bound.
No kernel may reach another device: no remote copies, remote signals or barrier semaphores. Data moves between devices by JAX's collectives and lax.ppermute only.
A program may use at most 64 MiB of HBM per device.

v0:
```python
import jax
import jax.numpy as jnp
from jax import lax
from jax.sharding import PartitionSpec as P


def per_device(encodings, label_weights, label_count, matched, positive):
    rows, width = encodings.shape
    top = matched.shape[1]
    local_clusters = label_count.shape[0]
    groups = lax.axis_size("grp")
    cluster_labels = lax.axis_size("dev")
    clusters = local_clusters * groups * cluster_labels
    labels = label_weights.shape[0] // local_clusters
    capacity = max(2, 3 * top * rows // (2 * clusters))
    items = rows * top
    flat_ids = matched.reshape(-1)
    order = jnp.argsort(flat_ids, stable=True)
    ordered = flat_ids[order]
    first = jnp.searchsorted(ordered, ordered, side="left")
    ranks_sorted = jnp.arange(items, dtype=jnp.int32) - first
    ranks = jnp.zeros((items,), jnp.int32).at[order].set(ranks_sorted)
    target_slot = flat_ids * capacity + ranks
    outgoing = jnp.zeros((clusters * capacity, width), jnp.bfloat16)
    outgoing = outgoing.at[target_slot].set(jnp.repeat(encodings, top, axis=0))
    wanted = jnp.zeros((clusters * capacity,), jnp.int32).at[target_slot].set(positive.reshape(-1))
    outgoing = outgoing.reshape(groups, cluster_labels, local_clusters, capacity, width)
    wanted = wanted.reshape(groups, cluster_labels, local_clusters, capacity)
    received_rows, slots = (
        lax.all_to_all(
            lax.all_to_all(outgoing, "grp", split_axis=0, concat_axis=0, tiled=True),
            "dev",
            split_axis=1,
            concat_axis=1,
            tiled=True,
        ),
        lax.all_to_all(
            lax.all_to_all(wanted, "grp", split_axis=0, concat_axis=0, tiled=True),
            "dev",
            split_axis=1,
            concat_axis=1,
            tiled=True,
        ),
    )
    label_blocks = label_weights.reshape(local_clusters, labels, width)
    label_scores = jnp.einsum(
        "eisof,suf->eisou", received_rows, label_blocks, preferred_element_type=jnp.float32
    )
    index = jnp.arange(labels, dtype=jnp.int32)
    valid = (index[None, :] < label_count[:, None])[None, None, :, None, :]
    target = (index == slots[..., None]).astype(jnp.float32)
    terms = jnp.where(
        valid, jax.nn.softplus(label_scores) - target * label_scores, jnp.float32(0.0)
    )
    slot_loss = jnp.sum(terms, axis=-1)
    encoding_gradient = jnp.where(
        valid, jax.nn.sigmoid(label_scores) - target, jnp.float32(0.0)
    ).astype(jnp.bfloat16)
    part_grad = jnp.einsum(
        "uahrq,hqz->uahrz", encoding_gradient, label_blocks, preferred_element_type=jnp.float32
    ).astype(jnp.bfloat16)
    label_weight_gradient = jnp.einsum(
        "utayz,utayp->azp", encoding_gradient, received_rows, preferred_element_type=jnp.float32
    )
    label_weight_gradient = label_weight_gradient.reshape(local_clusters * labels, width)
    returned, total_loss_value = (
        lax.all_to_all(
            lax.all_to_all(part_grad, "grp", split_axis=0, concat_axis=0, tiled=True),
            "dev",
            split_axis=1,
            concat_axis=1,
            tiled=True,
        ),
        lax.all_to_all(
            lax.all_to_all(
                slot_loss.astype(jnp.bfloat16), "grp", split_axis=0, concat_axis=0, tiled=True
            ),
            "dev",
            split_axis=1,
            concat_axis=1,
            tiled=True,
        ).astype(slot_loss.dtype),
    )
    picked = returned.reshape(clusters * capacity, width)[target_slot].reshape(rows, top, width)
    enc_grad = jnp.sum(picked.astype(jnp.float32), axis=1).astype(jnp.bfloat16)
    picked_loss = total_loss_value.reshape(-1)[target_slot].reshape(rows, top)
    query_loss = jnp.sum(picked_loss, axis=1) / (top * labels)
    return (enc_grad, query_loss, label_weight_gradient)


def solution(mesh):
    in_specs = (
        P(("grp", "dev"), None),
        P(("grp", "dev"), None),
        P(("grp", "dev")),
        P(("grp", "dev"), None),
        P(("grp", "dev"), None),
    )
    out_specs = (P(("grp", "dev"), None), P(("grp", "dev")), P(("grp", "dev"), None))
    return jax.shard_map(
        per_device, mesh=mesh, in_specs=in_specs, out_specs=out_specs, check_vma=False
    )
```

profile of v0, /device:TPU:2, one launch (start us, length us, event | category | flops | bytes accessed | tf_op | source)
XLA Modules:
  0.0 499.1 jit_solution(4609545327965486707)
XLA Ops:
  10.6 50.7 %while.25 = (s32[]{:T(128)}, u32[1024]{0:T(1024)S(1)}, u32[1024]{0:T(1024)S(1)}, s32[1024]{0:T(1024)S(1)}, s32[]{:T(128)}, /*index=5*/s32[]{:T(128)}, s32[]{}) while((s32[]{:T(128)}, u32[1024]{0:T(1024)S(1)}, u32[1024]{0:T(1024)S(1)}, s32[1024]{0:T(1024)S(1)}, s32[]{:T(128)}, /*index=5*/s32[]{:T(128)}, s32[]{}) %tuple.43), condition=%wide.region_2.3_spmd.clone, body=%wide.region_1.2_spmd.clone.sunk | while | flops 19460 | bytes 67685 | solution.py:20
  10.6 4.5 gather_fusion
  15.2 4.5 gather_fusion
  19.8 4.5 gather_fusion
  24.4 4.5 gather_fusion
  29.0 4.5 gather_fusion
  33.7 4.5 gather_fusion
  38.3 4.5 gather_fusion
  42.9 4.5 gather_fusion
  47.5 4.5 gather_fusion
  71.8 8.5 %all-to-all-start.2 = ((s32[8,1,256]{2,1,0:T(1,128)}), s32[8,1,256]{2,1,0:T(1,128)S(1)}, u32[]{:S(2)}, u32[]{:S(2)}) async-start(s32[8,1,256]{2,1,0:T(1,128)} %reshape.149), calls=%async_computation.2 | async-start | bytes 16384 | tf_op jit(solution)/shard_map/all_to_all | solution.py:38
  80.3 8.4 %scatter_custom_fusion.1 = bf16[2048,1024]{1,0:T(8,128)(2,1)} fusion(s32[1024]{0:T(1024)S(1)} %get-tuple-element.99, bf16[]{:T(256)} %constant.46.clone.1, bf16[128,1024]{1,0:T(8,128)(2,1)S(1)} %copy-done.1), kind=kCustom, calls=%fused_computation.18 | custom fusion | bytes 4456450 | tf_op jit(solution)/shard_map/scatter | solution.py:25
  88.6 7.2 %reshape.63 = bf16[8,32,4,2,1024]{4,3,2,1,0:T(2,128)(2,1)} reshape(bf16[2048,1024]{1,0:T(8,128)(2,1)} %scatter_custom_fusion.1) | data formatting | bytes 8388608 | tf_op jit(solution)/shard_map/reshape | solution.py:27
  95.9 7.9 %copy.30 = bf16[8,32,4,2,1024]{4,1,3,2,0:T(8,128)(2,1)} copy(bf16[8,32,4,2,1024]{4,3,2,1,0:T(2,128)(2,1)} %reshape.63) | data formatting | bytes 8388608 | tf_op jit(solution)/shard_map/reshape | solution.py:27
  103.8 7.2 %all-to-all-start = ((bf16[8,32,4,2,1024]{4,1,3,2,0:T(8,128)(2,1)}), bf16[8,32,4,2,1024]{4,1,3,2,0:T(8,128)(2,1)}, u32[]{:S(2)}, u32[]{:S(2)}) async-start(bf16[8,32,4,2,1024]{4,1,3,2,0:T(8,128)(2,1)} %copy.30), calls=%async_computation | async-start | bytes 8388608 | tf_op jit(solution)/shard_map/all_to_all | solution.py:31
  113.0 94.0 %all-to-all-done = bf16[8,32,4,2,1024]{4,1,3,2,0:T(8,128)(2,1)} async-done(((bf16[8,32,4,2,1024]{4,1,3,2,0:T(8,128)(2,1)}), bf16[8,32,4,2,1024]{4,1,3,2,0:T(8,128)(2,1)}, u32[]{:S(2)}, u32[]{:S(2)}) %all-to-all-start) | async-done | bytes 4194336 | tf_op jit(solution)/shard_map/all_to_all | solution.py:31
  207.0 7.6 %all-to-all-start.3 = ((s32[8,32,4,2]{0,2,3,1:T(4,128)}), s32[8,32,4,2]{0,2,3,1:T(4,128)S(1)}, u32[]{:S(2)}, u32[]{:S(2)}) async-start(s32[8,32,4,2]{0,2,3,1:T(4,128)} %copy.35), calls=%async_computation.3 | async-start | bytes 262144 | tf_op jit(solution)/shard_map/all_to_all | solution.py:37
  214.6 8.5 %copy.31 = bf16[8,32,4,2,1024]{4,3,0,2,1:T(2,128)(2,1)} copy(bf16[8,32,4,2,1024]{4,1,3,2,0:T(8,128)(2,1)} %all-to-all-done) | data formatting | bytes 8388608 | tf_op jit(solution)/shard_map/all_to_all | solution.py:31
  223.1 7.9 %all-to-all-start.1 = ((bf16[8,32,4,2,1024]{4,3,0,2,1:T(2,128)(2,1)}), bf16[8,32,4,2,1024]{4,3,0,2,1:T(2,128)(2,1)}, u32[]{:S(2)}, u32[]{:S(2)}) async-start(bf16[8,32,4,2,1024]{4,3,0,2,1:T(2,128)(2,1)} %copy.31), calls=%async_computation.1 | async-start | bytes 8388608 | tf_op jit(solution)/shard_map/all_to_all | solution.py:30
  231.2 51.0 %all-to-all-done.1 = bf16[8,32,4,2,1024]{4,3,0,2,1:T(2,128)(2,1)} async-done(((bf16[8,32,4,2,1024]{4,3,0,2,1:T(2,128)(2,1)}), bf16[8,32,4,2,1024]{4,3,0,2,1:T(2,128)(2,1)}, u32[]{:S(2)}, u32[]{:S(2)}) %all-to-all-start.1) | async-done | bytes 4194336 | tf_op jit(solution)/shard_map/all_to_all | solution.py:30
  282.2 6.3 %fusion.12 = (bf16[8,32,4,2]{1,3,0,2:T(2,128)(2,1)S(1)}, bf16[8,32,4,2,128]{4,1,3,0,2:T(8,128)(2,1)S(1)}) fusion(s32[8,32,4,2]{1,3,0,2:T(2,128)S(1)} %copy.36, pred[4,128]{1,0:T(4,128)(4,1)S(1)} %iota_compare_fusion.1, bf16[4,128,1024,1,1]{2,1,4,3,0:T(8,128)(2,1)S(1)} %bitcast.31, bf16[8,32,4,2,1024]{4,3,0,2,1:T(2,128)(2,1)} %all-to-all-done.1), kind=kOutput, calls=%fused_computation.24 | convolution fusion | flops 541587456 | bytes 5779968 | tf_op jit(solution)/shard_map/eisof,suf->eisou/dot_general | solution.py:46
  300.1 4.5 all-to-all-start.4
  305.5 94.4 %all-to-all-done.4 = bf16[8,32,4,2,1024]{4,1,3,2,0:T(8,128)(2,1)} async-done(((bf16[8,32,4,2,1024]{4,1,3,2,0:T(8,128)(2,1)}), bf16[8,32,4,2,1024]{4,1,3,2,0:T(8,128)(2,1)}, u32[]{:S(2)}, u32[]{:S(2)}) %all-to-all-start.4) | async-done | bytes 4194336 | tf_op jit(solution)/shard_map/all_to_all | solution.py:68
  399.9 5.5 %all-to-all-start.7 = ((bf16[8,32,4,2]{0,2,3,1:T(4,128)(2,1)}), bf16[8,32,4,2]{0,2,3,1:T(4,128)(2,1)S(1)}, u32[]{:S(2)}, u32[]{:S(2)}) async-start(bf16[8,32,4,2]{0,2,3,1:T(4,128)(2,1)} %copy.41), calls=%async_computation.7 | async-start | bytes 131072 | tf_op jit(solution)/shard_map/all_to_all | solution.py:74
  405.4 8.5 %copy.38 = bf16[8,32,4,2,1024]{4,3,0,2,1:T(2,128)(2,1)} copy(bf16[8,32,4,2,1024]{4,1,3,2,0:T(8,128)(2,1)} %all-to-all-done.4) | data formatting | bytes 8388608 | tf_op jit(solution)/shard_map/all_to_all | solution.py:68
  413.9 7.8 %all-to-all-start.5 = ((bf16[8,32,4,2,1024]{4,3,0,2,1:T(2,128)(2,1)}), bf16[8,32,4,2,1024]{4,3,0,2,1:T(2,128)(2,1)}, u32[]{:S(2)}, u32[]{:S(2)}) async-start(bf16[8,32,4,2,1024]{4,3,0,2,1:T(2,128)(2,1)} %copy.38), calls=%async_computation.5 | async-start | bytes 8388608 | tf_op jit(solution)/shard_map/all_to_all | solution.py:67
  421.8 6.2 %fusion = f32[4,128,1024,1,1]{2,1,4,0,3:T(8,128)} fusion(bf16[8,32,4,2,1024]{4,3,0,2,1:T(2,128)(2,1)} %all-to-all-done.1, bf16[8,32,4,2,128]{4,1,3,0,2:T(8,128)(2,1)S(1)} %get-tuple-element.101), kind=kOutput, calls=%fused_computation.11 | convolution fusion | flops 536870912 | bytes 6815744 | tf_op jit(solution)/shard_map/utayz,utayp->azp/dot_general | solution.py:62
  428.8 6.2 %gather_fusion.3 = f32[1024]{0:T(1024)S(1)} fusion(f32[2048]{0:T(1024)S(1)} %reshape.74, s32[1024]{0:T(1024)S(1)} %get-tuple-element.98), kind=kCustom, calls=%fused_computation.3 | custom fusion | bytes 12288 | tf_op jit(solution)/shard_map/gather | solution.py:86
  435.7 37.2 %all-to-all-done.5 = bf16[8,32,4,2,1024]{4,3,0,2,1:T(2,128)(2,1)} async-done(((bf16[8,32,4,2,1024]{4,3,0,2,1:T(2,128)(2,1)}), bf16[8,32,4,2,1024]{4,3,0,2,1:T(2,128)(2,1)}, u32[]{:S(2)}, u32[]{:S(2)}) %all-to-all-start.5) | async-done | bytes 4194336 | tf_op jit(solution)/shard_map/all_to_all | solution.py:67
  472.9 8.9 %copy.39 = bf16[8,32,4,2,1024]{4,3,2,1,0:T(2,128)(2,1)} copy(bf16[8,32,4,2,1024]{4,3,0,2,1:T(2,128)(2,1)} %all-to-all-done.5) | data formatting | bytes 8388608 | tf_op jit(solution)/shard_map/all_to_all | solution.py:67
  481.8 7.2 %reshape.67 = bf16[2048,1024]{1,0:T(8,128)(2,1)} reshape(bf16[8,32,4,2,1024]{4,3,2,1,0:T(2,128)(2,1)} %copy.39) | data formatting | bytes 8388608 | tf_op jit(solution)/shard_map/reshape | solution.py:84
  489.0 7.7 %gather_fusion.2 = bf16[1024,1024]{1,0:T(8,128)(2,1)S(1)} fusion(bf16[2048,1024]{1,0:T(8,128)(2,1)} %reshape.67, s32[1024]{0:T(1024)S(1)} %get-tuple-element.98), kind=kCustom, calls=%fused_computation.2 | custom fusion | bytes 4198400 | tf_op jit(solution)/shard_map/gather | solution.py:84
  (95 shorter events, 48.0 us)
Async XLA Ops:
  0.6 281.6 %copy-start = (bf16[512,1024]{1,0:T(8,128)(2,1)S(1)}, bf16[512,1024]{1,0:T(8,128)(2,1)}, u32[]{:S(2)}) copy-start(bf16[512,1024]{1,0:T(8,128)(2,1)} %param.8) | copy-start | bytes 3145732
  10.5 55.1 %copy-start.2 = (s32[128,8]{0,1:T(8,128)S(1)}, s32[128,8]{0,1:T(8,128)}, u32[]{:S(2)}) copy-start(s32[128,8]{0,1:T(8,128)} %param.11) | copy-start | bytes 12292
  10.6 69.7 %copy-start.1 = (bf16[128,1024]{1,0:T(8,128)(2,1)S(1)}, bf16[128,1024]{1,0:T(8,128)(2,1)}, u32[]{:S(2)}) copy-start(bf16[128,1024]{1,0:T(8,128)(2,1)} %param.7) | copy-start | bytes 786436
  71.8 32.0 %all-to-all-start.2 = ((s32[8,1,256]{2,1,0:T(1,128)}), s32[8,1,256]{2,1,0:T(1,128)S(1)}, u32[]{:S(2)}, u32[]{:S(2)}) async-start(s32[8,1,256]{2,1,0:T(1,128)} %reshape.149), calls=%async_computation.2 | async-start | bytes 16384 | tf_op jit(solution)/shard_map/all_to_all | solution.py:38
  103.8 103.2 %all-to-all-start = ((bf16[8,32,4,2,1024]{4,1,3,2,0:T(8,128)(2,1)}), bf16[8,32,4,2,1024]{4,1,3,2,0:T(8,128)(2,1)}, u32[]{:S(2)}, u32[]{:S(2)}) async-start(bf16[8,32,4,2,1024]{4,1,3,2,0:T(8,128)(2,1)} %copy.30), calls=%async_computation | async-start | bytes 8388608 | tf_op jit(solution)/shard_map/all_to_all | solution.py:31
  207.0 16.2 %all-to-all-start.3 = ((s32[8,32,4,2]{0,2,3,1:T(4,128)}), s32[8,32,4,2]{0,2,3,1:T(4,128)S(1)}, u32[]{:S(2)}, u32[]{:S(2)}) async-start(s32[8,32,4,2]{0,2,3,1:T(4,128)} %copy.35), calls=%async_computation.3 | async-start | bytes 262144 | tf_op jit(solution)/shard_map/all_to_all | solution.py:37
  223.1 7.9 %copy-start.3 = (s32[4]{0:T(128)S(1)}, s32[4]{0:T(128)}, u32[]{:S(2)}) copy-start(s32[4]{0:T(128)} %param.9) | copy-start | bytes 52
  223.1 59.1 %all-to-all-start.1 = ((bf16[8,32,4,2,1024]{4,3,0,2,1:T(2,128)(2,1)}), bf16[8,32,4,2,1024]{4,3,0,2,1:T(2,128)(2,1)}, u32[]{:S(2)}, u32[]{:S(2)}) async-start(bf16[8,32,4,2,1024]{4,3,0,2,1:T(2,128)(2,1)} %copy.31), calls=%async_computation.1 | async-start | bytes 8388608 | tf_op jit(solution)/shard_map/all_to_all | solution.py:30
  289.3 10.8 %all-to-all-start.6 = ((bf16[8,2,128]{2,1,0:T(2,128)(2,1)}), bf16[8,2,128]{2,1,0:T(2,128)(2,1)S(1)}, u32[]{:S(2)}, u32[]{:S(2)}) async-start(bf16[8,2,128]{2,1,0:T(2,128)(2,1)} %reshape.151), calls=%async_computation.6 | async-start | bytes 8192 | tf_op jit(solution)/shard_map/all_to_all | solution.py:75
  300.1 99.8 %all-to-all-start.4 = ((bf16[8,32,4,2,1024]{4,1,3,2,0:T(8,128)(2,1)}), bf16[8,32,4,2,1024]{4,1,3,2,0:T(8,128)(2,1)}, u32[]{:S(2)}, u32[]{:S(2)}) async-start(bf16[8,32,4,2,1024]{4,1,3,2,0:T(8,128)(2,1)} %copy.37), calls=%async_computation.4 | async-start | bytes 8388608 | tf_op jit(solution)/shard_map/all_to_all | solution.py:68
  399.9 14.0 %all-to-all-start.7 = ((bf16[8,32,4,2]{0,2,3,1:T(4,128)(2,1)}), bf16[8,32,4,2]{0,2,3,1:T(4,128)(2,1)S(1)}, u32[]{:S(2)}, u32[]{:S(2)}) async-start(bf16[8,32,4,2]{0,2,3,1:T(4,128)(2,1)} %copy.41), calls=%async_computation.7 | async-start | bytes 131072 | tf_op jit(solution)/shard_map/all_to_all | solution.py:74
  413.9 59.0 %all-to-all-start.5 = ((bf16[8,32,4,2,1024]{4,3,0,2,1:T(2,128)(2,1)}), bf16[8,32,4,2,1024]{4,3,0,2,1:T(2,128)(2,1)}, u32[]{:S(2)}, u32[]{:S(2)}) async-start(bf16[8,32,4,2,1024]{4,3,0,2,1:T(2,128)(2,1)} %copy.38), calls=%async_computation.5 | async-start | bytes 8388608 | tf_op jit(solution)/shard_map/all_to_all | solution.py:67
where the time goes:
time: 507 us; the launch traced here: 499 us
  waiting for transfers between devices  280 us (55%)
  local copies, waits for them, and re-layouts  143 us (28%)
  starting transfers between devices  52.4 us (10%)
  matrix products  13.8 us (3%)
  other arithmetic  8.19 us (2%)
    all_to_all x1, waiting for transfers between devices, per_device(): lax.all_to_all(part_grad, 'grp', split_axis=0, concat_axis=0, tiled=True)  94.4 us
    all_to_all x1, waiting for transfers between devices, per_device(): lax.all_to_all(outgoing, 'grp', split_axis=0, concat_axis=0, tiled=True)  94 us
    all_to_all x1, waiting for transfers between devices, per_device(): lax.all_to_all(lax.all_to_all(outgoing, 'grp', split_axis=0, concat_axis=...  51 us
    gather x11, local copies, waits for them, and re-layouts, per_device(): first = jnp.searchsorted(ordered, ordered, side='left')  49.8 us
    all_to_all x1, waiting for transfers between devices, per_device(): lax.all_to_all(lax.all_to_all(part_grad, 'grp', split_axis=0, concat_axis...  37.2 us
    reshape x2, local copies, waits for them, and re-layouts, per_device(): outgoing.reshape(groups, cluster_labels, local_clusters, capacity, width)  15.1 us
  transfers between devices with their start and end apart: 8, of which 5 were waited for; matrix products, arithmetic and copies ran while one was open for 12% of the time, Pallas kernels for 0%

commit v1 on v0

v1 whole, which is shorter than its diff:
```python
import functools

import jax
import jax.numpy as jnp
from jax import lax
from jax.experimental import pallas as pl
from jax.experimental.pallas import tpu as pltpu
from jax.sharding import PartitionSpec as P

F32 = jnp.float32
BF16 = jnp.bfloat16
EXTRA = 128
VMEM_LIMIT = 50 * 1024 * 1024


def iota(shape, dim):
    return lax.broadcasted_iota(jnp.int32, shape, dim)


def dispatch_kernel(grp_ref, x_ref, send_ref, pick_ref, *, top, per_dst):
    sources, queries, wide = x_ref.shape
    width = wide - EXTRA
    dsts = send_ref.shape[0]
    slots = 2 * per_dst
    rows = dsts * slots
    me = grp_ref[0].astype(F32)
    row = iota((rows, queries), 0)
    cluster = ((row // slots) * per_dst + row % per_dst).astype(F32)
    rank = ((row // per_dst) % 2).astype(F32)
    before = (iota((queries, queries), 0) < iota((queries, queries), 1)).astype(BF16)
    ones = jnp.ones((2 * queries, EXTRA), BF16)
    zero = jnp.zeros((dsts, slots, queries), F32)

    def one(source):
        meta = x_ref[source, :, width:].astype(F32).T
        group, local, slot = meta[0:top], meta[top : 2 * top], meta[2 * top : 3 * top]
        key = jnp.where(group == me, local, -1.0)
        want = slot + 1.0
        value = jnp.zeros((rows, queries), F32)
        for t in range(top):
            value = value + jnp.where(cluster == key[t : t + 1], want[t : t + 1], 0.0)
        hit = (value > 0.0).astype(BF16)
        earlier = jnp.dot(hit, before, preferred_element_type=F32)
        value = jnp.where(earlier == rank, value, 0.0)
        return value.reshape(dsts, slots, queries)

    for pair in range(sources // 2):
        a, b = one(2 * pair), one(2 * pair + 1)
        value = jnp.concatenate(
            [jnp.concatenate([a, zero], axis=2), jnp.concatenate([zero, b], axis=2)], axis=1
        ).reshape(2 * rows, 2 * queries)
        pick = (value > 0.0).astype(BF16)
        pick_ref[pair] = pick
        x = x_ref[2 * pair : 2 * pair + 2, :, 0:width].reshape(2 * queries, width)
        out = jnp.dot(pick, x, preferred_element_type=F32).astype(BF16)
        want = jnp.dot(value.astype(BF16), ones, preferred_element_type=F32).astype(BF16)
        at = pl.ds(pair * 2 * slots, 2 * slots)
        send_ref[:, at, 0:width] = out.reshape(dsts, 2 * slots, width)
        send_ref[:, at, width:] = want.reshape(dsts, 2 * slots, EXTRA)


def dispatch(x, grp, dsts, per_dst, top):
    sources, queries, wide = x.shape
    slots = sources * 2 * per_dst
    return pl.pallas_call(
        functools.partial(dispatch_kernel, top=top, per_dst=per_dst),
        out_shape=(
            jax.ShapeDtypeStruct((dsts, slots, wide), BF16),
            jax.ShapeDtypeStruct((sources // 2, dsts * 4 * per_dst, 2 * queries), BF16),
        ),
        in_specs=[pl.BlockSpec(memory_space=pltpu.SMEM), pl.BlockSpec(memory_space=pltpu.VMEM)],
        out_specs=[pl.BlockSpec(memory_space=pltpu.VMEM)] * 2,
        compiler_params=pltpu.CompilerParams(vmem_limit_bytes=VMEM_LIMIT),
        name="dispatch",
    )(grp, x)


def score_kernel(count_ref, x_ref, w_ref, ret_ref, grad_ref, *, per_dst):
    devs, slots, wide = x_ref.shape
    all_labels, width = w_ref.shape
    labels = all_labels // per_dst
    rows = devs * slots
    x = x_ref[...].reshape(rows, wide)
    want = x[:, width:].astype(F32)
    scores = lax.dot_general(
        x[:, 0:width], w_ref[...], (((1,), (1,)), ((), ())), preferred_element_type=F32
    )
    own = iota((rows, labels), 0) % per_dst
    label = iota((rows, labels), 1)
    s = scores[:, 0:labels]
    count = jnp.full((rows, labels), count_ref[0], jnp.int32)
    for cl in range(1, per_dst):
        s = jnp.where(own == cl, scores[:, cl * labels : (cl + 1) * labels], s)
        count = jnp.where(own == cl, count_ref[cl], count)
    valid = label < count
    target = (label.astype(F32) + 1.0) == want
    small = jnp.exp(-jnp.abs(s))
    soft = jnp.maximum(s, 0.0) + jnp.log1p(small)
    term = jnp.where(valid, soft - jnp.where(target, s, 0.0), 0.0)
    loss = jnp.sum(term, axis=1, keepdims=True)
    sig = jnp.where(s >= 0.0, 1.0, small) / (1.0 + small)
    grad = jnp.where(valid, sig - jnp.where(target, 1.0, 0.0), 0.0)
    wide_grad = jnp.concatenate(
        [jnp.where(own == cl, grad, 0.0) for cl in range(per_dst)], axis=1
    ).astype(BF16)
    grad_ref[...] = wide_grad
    part = jnp.dot(wide_grad, w_ref[...], preferred_element_type=F32).astype(BF16)
    ret_ref[:, :, 0:width] = part.reshape(devs, slots, width)
    ret_ref[:, :, width:] = (
        jnp.broadcast_to(loss, (rows, EXTRA)).astype(BF16).reshape(devs, slots, EXTRA)
    )


def score(x, weights, count, block):
    devs, slots, wide = x.shape
    per_dst = count.shape[0]
    all_labels, width = weights.shape
    return pl.pallas_call(
        functools.partial(score_kernel, per_dst=per_dst),
        grid=(devs // block,),
        out_shape=(
            jax.ShapeDtypeStruct((devs, slots, wide), BF16),
            jax.ShapeDtypeStruct((devs * slots, all_labels), BF16),
        ),
        in_specs=[
            pl.BlockSpec(memory_space=pltpu.SMEM),
            pl.BlockSpec((block, slots, wide), lambda i: (i, 0, 0)),
            pl.BlockSpec((all_labels, width), lambda i: (0, 0)),
        ],
        out_specs=[
            pl.BlockSpec((block, slots, wide), lambda i: (i, 0, 0)),
            pl.BlockSpec((block * slots, all_labels), lambda i: (i, 0)),
        ],
        compiler_params=pltpu.CompilerParams(vmem_limit_bytes=VMEM_LIMIT),
        name="score",
    )(count, x, weights)


def weight_kernel(x_ref, grad_ref, out_ref, *, width):
    devs, slots, wide = x_ref.shape
    x = x_ref[...].reshape(devs * slots, wide)[:, 0:width]
    part = lax.dot_general(
        grad_ref[...], x, (((0,), (0,)), ((), ())), preferred_element_type=F32
    )

    @pl.when(pl.program_id(0) == 0)
    def _():
        out_ref[...] = part

    @pl.when(pl.program_id(0) > 0)
    def _():
        out_ref[...] += part


def weight_gradient(x, grad, width, block):
    devs, slots, wide = x.shape
    all_labels = grad.shape[1]
    return pl.pallas_call(
        functools.partial(weight_kernel, width=width),
        grid=(devs // block,),
        out_shape=jax.ShapeDtypeStruct((all_labels, width), F32),
        in_specs=[
            pl.BlockSpec((block, slots, wide), lambda i: (i, 0, 0)),
            pl.BlockSpec((block * slots, all_labels), lambda i: (i, 0)),
        ],
        out_specs=pl.BlockSpec((all_labels, width), lambda i: (0, 0)),
        compiler_params=pltpu.CompilerParams(vmem_limit_bytes=VMEM_LIMIT),
        cost_estimate=pl.CostEstimate(
            flops=2 * devs * slots * all_labels * width,
            bytes_accessed=2 * devs * slots * (wide + all_labels) + 4 * all_labels * width,
            transcendentals=0,
        ),
        name="weight_gradient",
    )(x, grad)


def combine_kernel(ret_ref, pick_ref, out_ref):
    pairs, rows, _ = pick_ref.shape
    dsts, _, wide = ret_ref.shape
    two = rows // dsts
    for pair in range(pairs):
        x = ret_ref[:, pl.ds(pair * two, two), :].reshape(rows, wide)
        out = lax.dot_general(
            pick_ref[pair], x, (((0,), (0,)), ((), ())), preferred_element_type=F32
        )
        out_ref[pair] = out.astype(BF16)


def combine(ret, pick):
    pairs, rows, queries = pick.shape
    wide = ret.shape[2]
    return pl.pallas_call(
        combine_kernel,
        out_shape=jax.ShapeDtypeStruct((pairs, queries, wide), BF16),
        in_specs=[pl.BlockSpec(memory_space=pltpu.VMEM)] * 2,
        out_specs=pl.BlockSpec(memory_space=pltpu.VMEM),
        compiler_params=pltpu.CompilerParams(vmem_limit_bytes=VMEM_LIMIT),
        name="combine",
    )(ret, pick)


def per_device(encodings, label_weights, label_count, matched, positive):
    queries, width = encodings.shape
    top = matched.shape[1]
    per_dst = label_count.shape[0]
    dsts = lax.axis_size("dev")
    groups = lax.axis_size("grp")
    in_group = per_dst * dsts
    labels = label_weights.shape[0] // per_dst
    meta = jnp.concatenate([matched // in_group, matched % in_group, positive], axis=1).astype(BF16)
    meta = jnp.pad(meta, ((0, 0), (0, EXTRA - 3 * top)))
    own = jnp.concatenate([encodings, meta], axis=1)
    gathered = lax.all_gather(own, "grp", axis=0, tiled=False)
    me = lax.axis_index("grp").astype(jnp.int32).reshape(1)
    send, pick = dispatch(gathered, me, dsts, per_dst, top)
    received = lax.all_to_all(send, "dev", split_axis=0, concat_axis=0, tiled=True)
    part, grad = score(received, label_weights, label_count, min(8, dsts))
    returned = lax.all_to_all(part, "dev", split_axis=0, concat_axis=0, tiled=True)
    weight_grad = weight_gradient(received, grad, width, min(8, dsts))
    partial = combine(returned, pick).reshape(groups * queries, width + EXTRA)
    total = lax.psum_scatter(partial, "grp", scatter_dimension=0, tiled=True)
    enc_grad = total[:, 0:width]
    query_loss = total[:, width].astype(F32) / (top * labels)
    return enc_grad, query_loss, weight_grad


def solution(mesh):
    in_specs = (
        P(("grp", "dev"), None),
        P(("grp", "dev"), None),
        P(("grp", "dev")),
        P(("grp", "dev"), None),
        P(("grp", "dev"), None),
    )
    out_specs = (P(("grp", "dev"), None), P(("grp", "dev")), P(("grp", "dev"), None))
    return jax.shard_map(
        per_device, mesh=mesh, in_specs=in_specs, out_specs=out_specs, check_vma=False
    )
```

time: 507 us -> 251 us (0.50); the launches traced: 499 us -> 250 us
  waiting for transfers between devices: 280 us -> 78 us
  local copies, waits for them, and re-layouts: 143 us -> 3.46 us
  blocking collectives: 0 us -> 125 us
  starting transfers between devices: 52.4 us -> 0.08 us
  Pallas kernels: 0 us -> 25.6 us
  matrix products: 13.8 us -> 0 us
  between operations: 1.11 us -> 14 us
    all_to_all x8 -> x0, waiting for transfers between devices: 280 us -> none  [the longest x1 94.4 us: per_device(): lax.all_to_all(part_grad, 'grp', split_axis=0, concat_axis=0, tiled=True)]
    all_to_all x0 -> x2, blocking collectives: none -> 125 us  [the longest x1 63.1 us: per_device(): lax.all_to_all(send, 'dev', split_axis=0, concat_axis=0, tiled=True)]
    gather x14 -> x0, local copies, waits for them, and re-layouts: 68.2 us -> none  [the longest x11 49.8 us: per_device(): first = jnp.searchsorted(ordered, ordered, side='left')]
    all_to_all x8 -> x0, starting transfers between devices: 52.4 us -> none  [the longest x1 8.47 us: per_device(): lax.all_to_all(wanted, 'grp', split_axis=0, concat_axis=0, tiled=True)]
    all_gather x0 -> x1, waiting for transfers between devices: none -> 44.6 us  [per_device(): gathered = lax.all_gather(own, 'grp', axis=0, tiled=False)]
    reduce_scatter x0 -> x1, waiting for transfers between devices: none -> 33.4 us  [per_device(): total = lax.psum_scatter(partial, 'grp', scatter_dimension=0, tiled=True)]
    all_to_all x8 -> x0, local copies, waits for them, and re-layouts: 28.2 us -> none  [the longest x1 8.9 us: per_device(): lax.all_to_all(lax.all_to_all(part_grad, 'grp', split_axis=0, concat_axis...]
    pallas_call x0 -> x4, Pallas kernels: none -> 25.6 us  [the longest x1 8.96 us: score(): pl.pallas_call(functools.partial(score_kernel, per_dst=per_dst), grid=(de...]
  transfers between devices with their start and end apart: 8 -> 2, of which waited for: 5 -> 2; matrix products, arithmetic and copies ran while one was open for 12% -> 0% of each run, Pallas kernels for 0% -> 3%
where the time goes in v1:
time: 251 us; the launch traced here: 250 us
  blocking collectives  125 us (50%)
  waiting for transfers between devices  78 us (31%)
  Pallas kernels  25.6 us (10%)
  between operations  14 us (6%)
  other arithmetic  4.47 us (2%)
  local copies, waits for them, and re-layouts  3.46 us (1%)
    all_to_all x1, blocking collectives, per_device(): lax.all_to_all(send, 'dev', split_axis=0, concat_axis=0, tiled=True)  63.1 us
    all_to_all x1, blocking collectives, per_device(): lax.all_to_all(part, 'dev', split_axis=0, concat_axis=0, tiled=True)  61.6 us
    all_gather x1, waiting for transfers between devices, per_device(): gathered = lax.all_gather(own, 'grp', axis=0, tiled=False)  44.6 us
    reduce_scatter x1, waiting for transfers between devices, per_device(): total = lax.psum_scatter(partial, 'grp', scatter_dimension=0, tiled=True)  33.4 us
    pallas_call x1, Pallas kernels, score(): pl.pallas_call(functools.partial(score_kernel, per_dst=per_dst), grid=(de...  8.96 us
    pallas_call x1, Pallas kernels, weight_gradient(): pl.pallas_call(functools.partial(weight_kernel, width=width), grid=(devs...  6.72 us
    pallas_call x1, Pallas kernels, combine(): pl.pallas_call(combine_kernel, out_shape=jax.ShapeDtypeStruct((pairs, que...  5.27 us
  transfers between devices with their start and end apart: 2, of which 2 were waited for; matrix products, arithmetic and copies ran while one was open for 0% of the time, Pallas kernels for 3%

profile of v1, /device:TPU:2, one launch (start us, length us, event | category | flops | bytes accessed | tf_op | source)
XLA Modules:
  0.0 250.3 jit_solution(1177023797055469)
XLA Ops:
  7.2 0.0 all-gather.3.cloned.1.call-start
  7.2 0.7 convert.11
  7.9 0.7 fusion.2
  8.6 0.1 copy.10
  8.7 1.7 fusion.1
  10.4 0.0 all-gather.3.cloned.1.call-update
  10.4 0.0 reduce-scatter.2.cloned.1.call-start
  10.5 44.6 %all-gather.3.cloned.1.call-done = bf16[1024,1152]{1,0:T(8,128)(2,1)} async-done(((bf16[128,1152]{1,0:T(8,128)(2,1)}), bf16[1024,1152]{1,0:T(8,128)(2,1)}) %all-gather.3.cloned.1.call-update) | async-done | bytes 2359312 | tf_op jit(solution)/shard_map/all_gather | solution.py:213
  55.1 0.0 copy-start
  55.1 1.7 copy-done
  56.8 4.6 %dispatch.1 = (bf16[32,64,1152]{2,1,0:T(8,128)(2,1)}, bf16[4,512,256]{2,1,0:T(8,128)(2,1)S(1)}) custom-call(s32[1]{0:T(128)} %bitcast.grp_ref, bf16[8,128,1152]{2,1,0:T(8,128)(2,1)S(1)} %bitcast.3), custom_call_target="tpu_custom_call" | custom-call | tf_op jit(solution)/shard_map/dispatch/pallas_call | solution.py:65
  61.4 0.0 copy-start.1
  61.4 0.0 copy-start.2
  61.4 63.1 %all_to_all.10.x_ref = bf16[32,64,1152]{2,1,0:T(8,128)(2,1)} all-to-all(bf16[32,64,1152]{2,1,0:T(8,128)(2,1)} %get-tuple-element.7), channel_id=1, replica_groups=mesh['grp'=8,'dev'=32] {'dev'}, dimensions={0} | all-to-all | bytes 9437184 | tf_op jit(solution)/shard_map/all_to_all | solution.py:216
  124.5 0.0 copy-done.1
  124.5 0.0 copy-done.2
  124.5 9.0 %score.1 = (bf16[32,64,1152]{2,1,0:T(8,128)(2,1)}, bf16[2048,512]{1,0:T(8,128)(2,1)S(1)}) custom-call(s32[4]{0:T(128)S(1)} %copy-done.2, bf16[32,64,1152]{2,1,0:T(8,128)(2,1)} %all_to_all.10.x_ref, bf16[512,1024]{1,0:T(8,128)(2,1)S(1)} %copy-done.1), custom_call_target="tpu_custom_call" | custom-call | tf_op jit(solution)/shard_map/score/pallas_call | solution.py:118
  133.5 61.6 %all_to_all.11.ret_ref = bf16[32,64,1152]{2,1,0:T(8,128)(2,1)} all-to-all(bf16[32,64,1152]{2,1,0:T(8,128)(2,1)} %get-tuple-element.8), channel_id=1, replica_groups=mesh['grp'=8,'dev'=32] {'dev'}, dimensions={0} | all-to-all | bytes 9437184 | tf_op jit(solution)/shard_map/all_to_all | solution.py:218
  195.0 5.3 %combine.1 = bf16[4,256,1152]{2,1,0:T(8,128)(2,1)} custom-call(bf16[32,64,1152]{2,1,0:T(8,128)(2,1)} %all_to_all.11.ret_ref, bf16[4,512,256]{2,1,0:T(8,128)(2,1)S(1)} %get-tuple-element.9.pick_ref), custom_call_target="tpu_custom_call" | custom-call | tf_op jit(solution)/shard_map/combine/pallas_call | solution.py:192
  200.3 0.0 reduce-scatter.2.cloned.1.call-update
  200.3 6.7 %weight_gradient.1 = f32[512,1024]{1,0:T(8,128)} custom-call(bf16[32,64,1152]{2,1,0:T(8,128)(2,1)} %all_to_all.10.x_ref, bf16[2048,512]{1,0:T(8,128)(2,1)S(1)} %get-tuple-element.10.grad_ref), custom_call_target="tpu_custom_call" | custom-call | flops 2147483648 | bytes 8912896 | tf_op jit(solution)/shard_map/weight_gradient/pallas_call | solution.py:158
  207.1 33.4 %reduce-scatter.2.cloned.1.call-done = bf16[128,1152]{1,0:T(8,128)(2,1)} async-done(((bf16[1024,1152]{1,0:T(8,128)(2,1)}), bf16[128,1152]{1,0:T(8,128)(2,1)}) %reduce-scatter.2.cloned.1.call-update) | async-done | bytes 294928 | tf_op jit(solution)/shard_map/reduce_scatter | solution.py:221
  240.4 1.4 multiply_reduce_fusion
  241.8 1.7 slice.8
  (1 shorter events, 0.0 us)
Async XLA Ops:
  7.2 48.0 %all-gather.3.cloned.1.call-start = ((), (), s32[]{:S(2)}) async-start(), calls=%async_computation.4 | async-start | bytes 2654208 | tf_op jit(solution)/shard_map/all_gather | solution.py:213
  10.4 230.0 %reduce-scatter.2.cloned.1.call-start = ((), (), s32[]{:S(2)}) async-start(), calls=%async_computation.3 | async-start | bytes 2654208 | tf_op jit(solution)/shard_map/reduce_scatter | solution.py:221
  55.1 1.7 copy-start
  61.4 63.1 %copy-start.1 = (bf16[512,1024]{1,0:T(8,128)(2,1)S(1)}, bf16[512,1024]{1,0:T(8,128)(2,1)}, u32[]{:S(2)}) copy-start(bf16[512,1024]{1,0:T(8,128)(2,1)} %w_ref.1) | copy-start | bytes 3145732
  61.4 63.1 %copy-start.2 = (s32[4]{0:T(128)S(1)}, s32[4]{0:T(128)}, u32[]{:S(2)}) copy-start(s32[4]{0:T(128)} %count_ref.1) | copy-start | bytes 52
Sparse Core Ops, SparseCore 0:
  10.6 44.5 all-gather.2
  200.5 39.9 reduce-scatter.1

commit v2 on v1

v2 whole, which is shorter than its diff:
```python
import functools

import jax
import jax.numpy as jnp
from jax import lax
from jax.experimental import pallas as pl
from jax.experimental.pallas import tpu as pltpu
from jax.sharding import PartitionSpec as P

F32 = jnp.float32
BF16 = jnp.bfloat16
LANES = 128
TILE = 8
META = 16
PARAMS = pltpu.CompilerParams(vmem_limit_bytes=63 * 1024 * 1024)
SMALL = pltpu.CompilerParams(vmem_limit_bytes=28 * 1024 * 1024)
IN_HBM = pl.BlockSpec(memory_space=pltpu.HBM)
IN_VMEM = pl.BlockSpec(memory_space=pltpu.VMEM)


def iota(shape, dim):
    return lax.broadcasted_iota(jnp.int32, shape, dim)


def whole(shape):
    return pl.BlockSpec(shape, lambda i: (0,) * len(shape))


def unit_row(row):
    return (iota((LANES, LANES), 0) == row).astype(BF16)


def unit_column(shape, column):
    return (iota(shape, 1) == column).astype(BF16)


def store_tiles(ref, first, rows, at=slice(None)):
    for k in range(0, rows.shape[2] // LANES, 2):
        left = rows[:, :, k * LANES : (k + 1) * LANES]
        right = rows[:, :, (k + 1) * LANES : (k + 2) * LANES]
        ref[at, pl.ds(first + k * TILE, 2 * TILE), :] = jnp.concatenate([left, right], axis=1).astype(BF16)


def load_tiles(held, width):
    devs, tile_rows, _ = held.shape
    per_source = width // LANES
    sources = (tile_rows // TILE - 1) // per_source
    tiles = held.astype(F32).reshape(devs, tile_rows // TILE, TILE, LANES)
    rows = [
        jnp.concatenate([tiles[:, s * per_source + k] for k in range(per_source)], axis=2)
        for s in range(sources)
    ]
    return rows, tiles[:, sources * per_source].reshape(devs * TILE, LANES).astype(BF16)


def prepare_kernel(enc_ref, matched_ref, positive_ref, out_ref, held, sems, *, in_group):
    queries = enc_ref.shape[0]
    top = matched_ref.shape[0]
    copies = [
        pltpu.make_async_copy(matched_ref, held.at[0], sems.at[0]),
        pltpu.make_async_copy(positive_ref, held.at[1], sems.at[1]),
        pltpu.make_async_copy(enc_ref, out_ref.at[pl.ds(0, queries)], sems.at[2]),
    ]
    for copy in copies:
        copy.start()
    copies[0].wait()
    copies[1].wait()
    matched = held[0]
    group = matched // in_group
    parts = (group, matched - group * in_group, held[1])
    meta = jnp.concatenate([part.astype(F32) for part in parts], axis=1)
    meta = jnp.concatenate([meta, jnp.zeros((top, out_ref.shape[1] - meta.shape[1]), F32)], axis=1)
    meta = jnp.concatenate([meta, jnp.zeros((META - top, meta.shape[1]), F32)], axis=0)
    out_ref[queries:] = meta.astype(BF16)
    copies[2].wait()


def prepare(encodings, matched, positive, in_group):
    queries, width = encodings.shape
    top = matched.shape[1]
    return pl.pallas_call(
        functools.partial(prepare_kernel, in_group=in_group),
        out_shape=jax.ShapeDtypeStruct((queries + META, width), BF16),
        in_specs=[IN_HBM] * 3,
        out_specs=IN_VMEM,
        scratch_shapes=[pltpu.VMEM((2, top, queries), jnp.int32), pltpu.SemaphoreType.DMA((3,))],
        compiler_params=PARAMS,
        name="prepare",
    )(encodings, matched.T, positive.T)


def dispatch_kernel(grp_ref, *refs, parts, top, per_dst, steps):
    x_refs, (send_ref, pick_ref, send, picks, sems) = refs[:-5], refs[-5:]
    width = x_refs[0].shape[1]
    queries = pick_ref.shape[2]
    sources = len(parts)
    dsts = send_ref.shape[0] // steps
    rows = dsts * TILE
    me = grp_ref[0].astype(F32)
    row = iota((rows, queries), 0)
    rank = ((row // per_dst) % 2).astype(F32)
    before = (iota((queries, queries), 0) < iota((queries, queries), 1)).astype(BF16)
    blocks, keys, wants, first = [], [], [], 0
    for count in parts:
        x = jnp.concatenate([r[...] for r in x_refs[first : first + count]], axis=0)
        first += count
        meta = x[queries:].astype(F32)[0:top]
        group, local, slot = [meta[:, i * queries : (i + 1) * queries] for i in range(3)]
        blocks.append(x[0:queries])
        keys.append(jnp.where(group == me, local, -1.0).astype(BF16))
        wants.append((slot + 1.0).astype(BF16))
    copies = []
    for step in range(steps):
        cluster = ((row // TILE + step * dsts) * per_dst + row % per_dst).astype(F32).astype(BF16)
        at, at_rows = pl.ds(step * dsts, dsts), pl.ds(step * rows, rows)
        last = jnp.zeros((rows, LANES), F32)
        for source in range(sources):
            value = jnp.zeros((rows, queries), BF16)
            for t in range(top):
                same = cluster == keys[source][t : t + 1]
                value = value + jnp.where(same, wants[source][t : t + 1], jnp.zeros((), BF16))
            hit = (value > 0.0).astype(BF16)
            earlier = jnp.dot(hit, before, preferred_element_type=F32)
            value = jnp.where(earlier == rank, value.astype(F32), 0.0)
            pick = (value > 0.0).astype(BF16)
            picks[source, at_rows, :] = pick
            out = jnp.dot(pick, blocks[source], preferred_element_type=F32)
            store_tiles(send, source * width // LANES * TILE, out.reshape(dsts, TILE, width), at)
            place = unit_column((queries, LANES), source)
            last = last + jnp.dot(value.astype(BF16), place, preferred_element_type=F32)
        end = sources * width // LANES * TILE
        send[at, end:, :] = last.reshape(dsts, TILE, LANES).astype(BF16)
        copies.append(pltpu.make_async_copy(send.at[at], send_ref.at[at], sems.at[0, step]))
        copies.append(
            pltpu.make_async_copy(picks.at[:, at_rows], pick_ref.at[:, at_rows], sems.at[1, step])
        )
        copies[-2].start()
        copies[-1].start()
    for copy in copies:
        copy.wait()


def dispatch(sources, grp, dsts, per_dst, top):
    flat = [block for blocks in sources for block in blocks]
    queries = sum(block.shape[0] for block in sources[0]) - META
    width = flat[0].shape[1]
    send = (dsts, (len(sources) * width // LANES + 1) * TILE, LANES)
    pick = (len(sources), dsts * TILE, queries)
    steps = 2
    return pl.pallas_call(
        functools.partial(
            dispatch_kernel,
            parts=[len(blocks) for blocks in sources],
            top=top,
            per_dst=per_dst,
            steps=steps,
        ),
        out_shape=(jax.ShapeDtypeStruct(send, BF16), jax.ShapeDtypeStruct(pick, BF16)),
        in_specs=[pl.BlockSpec(memory_space=pltpu.SMEM)] + [IN_VMEM] * len(flat),
        out_specs=[IN_HBM, IN_HBM],
        scratch_shapes=[
            pltpu.VMEM(send, BF16),
            pltpu.VMEM(pick, BF16),
            pltpu.SemaphoreType.DMA((2, steps)),
        ],
        compiler_params=SMALL,
        name="dispatch",
    )(grp, *flat)


def own_columns(grad, per_dst):
    own = iota(grad.shape, 0) % per_dst
    return jnp.concatenate([jnp.where(own == cl, grad, 0.0) for cl in range(per_dst)], axis=1).astype(BF16)


def score_kernel(count_ref, x_ref, w_ref, *refs, per_dst, carried, outs):
    carry_ref, ret_refs, grad_ref = refs[0], refs[1 if carried else 0 : -1], refs[-1]
    devs = x_ref.shape[0]
    all_labels, width = w_ref.shape
    labels = all_labels // per_dst
    per_source = width // LANES * TILE
    tiles, last = load_tiles(x_ref[...], width)
    sources = len(tiles)
    rows = devs * sources * TILE
    x = jnp.concatenate([t.reshape(devs, 1, TILE, width) for t in tiles], axis=1)
    x = x.reshape(rows, width).astype(BF16)
    want = jnp.concatenate(
        [
            jnp.dot(last, unit_row(s), preferred_element_type=F32).reshape(devs, 1, TILE, LANES)
            for s in range(sources)
        ],
        axis=1,
    ).reshape(rows, LANES)
    scores = lax.dot_general(
        x, w_ref[...], (((1,), (1,)), ((), ())), preferred_element_type=F32
    )
    own = iota((rows, labels), 0) % per_dst
    label = iota((rows, labels), 1)
    s = scores[:, 0:labels]
    count = jnp.full((rows, labels), count_ref[0], jnp.int32)
    for cl in range(1, per_dst):
        s = jnp.where(own == cl, scores[:, cl * labels : (cl + 1) * labels], s)
        count = jnp.where(own == cl, count_ref[cl], count)
    valid = label < count
    target = (label.astype(F32) + 1.0) == want
    small = jnp.exp(-jnp.abs(s))
    soft = jnp.maximum(s, 0.0) + jnp.log(1.0 + small)
    term = jnp.where(valid, soft - jnp.where(target, s, 0.0), 0.0)
    loss = jnp.sum(term, axis=1, keepdims=True).reshape(devs, sources, TILE, 1)
    sig = jnp.where(s >= 0.0, 1.0, small) / (1.0 + small)
    grad = jnp.where(valid, sig - jnp.where(target, 1.0, 0.0), 0.0)
    grad_ref[...] = grad.astype(BF16)
    part = jnp.dot(own_columns(grad, per_dst), w_ref[...], preferred_element_type=F32)
    part = part.reshape(devs, sources, TILE, width)
    lane = iota((devs, TILE, LANES), 2)
    for i, (ret_ref, members) in enumerate(zip(ret_refs, outs)):
        before = carried if i == 0 else 0
        last = jnp.zeros((devs, TILE, LANES), F32)
        if before:
            end = before * per_source
            ret_ref[:, 0:end, :] = carry_ref[:, 0:end, :]
            last = carry_ref[:, end:, :].astype(F32)
        for j, source in enumerate(members):
            store_tiles(ret_ref, (before + j) * per_source, part[:, source])
            last = jnp.where(lane == before + j, loss[:, source], last)
        ret_ref[:, (before + len(members)) * per_source :, :] = last.astype(BF16)


def sources_of(x, width):
    return (x.shape[1] // TILE - 1) * LANES // width


def score(x, weights, count, block, outs, carry=None):
    devs, tile_rows, _ = x.shape
    per_dst = count.shape[0]
    all_labels, width = weights.shape
    labels = all_labels // per_dst
    slots = sources_of(x, width) * TILE
    carried = sources_of(carry, width) if carry is not None else 0
    sizes = [len(members) + (carried if i == 0 else 0) for i, members in enumerate(outs)]
    ret_rows = [(size * width // LANES + 1) * TILE for size in sizes]

    def by_dev(rows):
        return pl.BlockSpec((block, rows, LANES), lambda i: (i, 0, 0))

    return pl.pallas_call(
        functools.partial(score_kernel, per_dst=per_dst, carried=carried, outs=outs),
        grid=(devs // block,),
        out_shape=[jax.ShapeDtypeStruct((devs, r, LANES), BF16) for r in ret_rows]
        + [jax.ShapeDtypeStruct((devs * slots, labels), BF16)],
        in_specs=[
            pl.BlockSpec(memory_space=pltpu.SMEM),
            by_dev(tile_rows),
            whole((all_labels, width)),
        ]
        + ([by_dev(carry.shape[1])] if carried else []),
        out_specs=[by_dev(r) for r in ret_rows]
        + [pl.BlockSpec((block * slots, labels), lambda i: (i, 0))],
        compiler_params=PARAMS,
        cost_estimate=pl.CostEstimate(
            flops=4 * devs * slots * all_labels * width,
            bytes_accessed=4 * devs * slots * (width + labels) + 2 * all_labels * width,
            transcendentals=0,
        ),
        name="score",
    )(count, x, weights, *([carry] if carried else []))


def weight_kernel(*refs, per_dst):
    out_ref = refs[-1]
    width = out_ref.shape[1]
    total = None
    for x_ref, grad_ref in zip(refs[0:-1:2], refs[1:-1:2]):
        tiles, _ = load_tiles(x_ref[...], width)
        devs = x_ref.shape[0]
        x = jnp.concatenate([t.reshape(devs, 1, TILE, width) for t in tiles], axis=1)
        x = x.reshape(devs * len(tiles) * TILE, width).astype(BF16)
        grad = own_columns(grad_ref[...].astype(F32), per_dst)
        part = lax.dot_general(
            grad, x, (((0,), (0,)), ((), ())), preferred_element_type=F32
        )
        total = part if total is None else total + part

    @pl.when(pl.program_id(0) == 0)
    def _():
        out_ref[...] = total

    @pl.when(pl.program_id(0) > 0)
    def _():
        out_ref[...] += total


def weight_gradient(chunks, width, block, per_dst):
    labels = chunks[0][1].shape[1]
    all_labels = labels * per_dst
    devs = chunks[0][0].shape[0]
    rows = sum(grad.shape[0] for _, grad in chunks)
    flat = [a for chunk in chunks for a in chunk]
    specs = []
    for x, grad in chunks:
        specs.append(pl.BlockSpec((block,) + x.shape[1:], lambda i: (i, 0, 0)))
        specs.append(pl.BlockSpec((grad.shape[0] * block // devs, labels), lambda i: (i, 0)))
    return pl.pallas_call(
        functools.partial(weight_kernel, per_dst=per_dst),
        grid=(devs // block,),
        out_shape=jax.ShapeDtypeStruct((all_labels, width), F32),
        in_specs=specs,
        out_specs=whole((all_labels, width)),
        compiler_params=PARAMS,
        cost_estimate=pl.CostEstimate(
            flops=2 * rows * all_labels * width,
            bytes_accessed=2 * rows * (width + all_labels) + 4 * all_labels * width,
            transcendentals=0,
        ),
        name="weight_gradient",
    )(*flat)


def combine_kernel(ret_ref, *refs, order, picks, parts, added, width, steps):
    pick_refs, refs = refs[:picks], refs[picks:]
    add_refs, refs = dict(zip(added, refs[: len(added)])), refs[len(added) :]
    out_refs, ret = refs[: sum(parts)], refs[sum(parts)]
    held, sems = refs[sum(parts) + 1 : -1], refs[-1]
    dsts = ret_ref.shape[0] // steps
    queries = held[0].shape[2]
    rows = dsts * TILE
    over_rows = (((0,), (0,)), ((), ()))
    ats = [pl.ds(step * dsts, dsts) for step in range(steps)]
    pick_copies = [
        pltpu.make_async_copy(ref, place, sems.at[steps + i])
        for i, (ref, place) in enumerate(zip(pick_refs, held))
    ]
    ret_copies = [
        pltpu.make_async_copy(ret_ref.at[at], ret.at[at], sems.at[step]) for step, at in enumerate(ats)
    ]
    for copy in pick_copies + ret_copies:
        copy.start()
    for copy in pick_copies:
        copy.wait()
    totals = [None] * len(order)
    for step, at in enumerate(ats):
        ret_copies[step].wait()
        tiles, last = load_tiles(ret[at], width)
        for source, (which, index) in enumerate(order):
            pick = held[which][index, pl.ds(step * rows, rows), :]
            x = tiles[source].reshape(rows, width).astype(BF16)
            loss = jnp.dot(last, unit_row(source), preferred_element_type=F32).astype(BF16)
            x = jnp.concatenate([x, loss], axis=1)
            out = lax.dot_general(pick, x, over_rows, preferred_element_type=F32)
            totals[source] = out if step == 0 else totals[source] + out
    first = 0
    for source, count in enumerate(parts):
        out = totals[source]
        if source in add_refs:
            out = out + add_refs[source][...].astype(F32)
        part = queries // count
        for i in range(count):
            out_refs[first + i][...] = out[i * part : (i + 1) * part].astype(BF16)
        first += count


def combine(ret, picks, order, parts, width, arrived=(), params=SMALL):
    queries = picks[0].shape[2]
    shapes = [(queries // count, width + LANES) for count in parts for _ in range(count)]
    added = [a for _, a in arrived]
    steps = 2
    return pl.pallas_call(
        functools.partial(
            combine_kernel,
            order=order,
            picks=len(picks),
            parts=parts,
            added=[i for i, _ in arrived],
            width=width,
            steps=steps,
        ),
        out_shape=[jax.ShapeDtypeStruct(shape, BF16) for shape in shapes],
        in_specs=[IN_HBM] * (1 + len(picks)) + [IN_VMEM] * len(added),
        out_specs=[IN_VMEM] * len(shapes),
        scratch_shapes=[pltpu.VMEM(ret.shape, BF16)]
        + [pltpu.VMEM(pick.shape, BF16) for pick in picks]
        + [pltpu.SemaphoreType.DMA((steps + len(picks),))],
        compiler_params=params,
        name="combine",
    )(ret, *picks, *added)


def add(a, b):
    return (a.astype(F32) + b.astype(F32)).astype(BF16)


def add_half(a, half, second):
    zero = jnp.zeros_like(half)
    return add(a, jnp.concatenate([zero, half] if second else [half, zero], axis=0))


def per_device(encodings, label_weights, label_count, matched, positive):
    queries, width = encodings.shape
    top = matched.shape[1]
    per_dst = label_count.shape[0]
    dsts = lax.axis_size("dev")
    groups = lax.axis_size("grp")
    labels = label_weights.shape[0] // per_dst
    half = queries // 2
    reach = groups // 2
    up_pairs = [(i, (i + 1) % groups) for i in range(groups)]
    down_pairs = [(i, (i - 1) % groups) for i in range(groups)]

    def up(v):
        return lax.ppermute(v, "grp", up_pairs)

    def down(v):
        return lax.ppermute(v, "grp", down_pairs)

    def exchange(v):
        return lax.all_to_all(v, "dev", split_axis=0, concat_axis=0, tiled=True)

    me = lax.axis_index("grp").astype(jnp.int32).reshape(1)
    own = prepare(encodings, matched, positive, per_dst * dsts)
    lower, upper = [own], [own]
    for _ in range(1, reach):
        lower.append(up(lower[-1]))
        upper.append(down(upper[-1]))
    across = (up(lower[-1][:half]), down(upper[-1][half:]))
    chunks = [
        [(own,)],
        [(v[k],) for k in range(1, reach - 1) for v in (lower, upper)],
        [(lower[-1],), (upper[-1],), across],
    ]
    picks, got = [], []
    for sources in chunks:
        send, pick = dispatch(sources, me, dsts, per_dst, top)
        if got:
            send, got[-1] = lax.optimization_barrier((send, got[-1]))
        got.append(exchange(send))
        picks.append(pick)

    block = min(16, dsts)
    mid = list(range(len(chunks[1])))
    part_own, grad_own = score(got[0], label_weights, label_count, block, [[0]])
    part_near, part_mid, grad_mid = score(
        got[1], label_weights, label_count, block, [mid[:2], mid[2:]], part_own
    )
    part_mid, part_near = lax.optimization_barrier((part_mid, part_near))
    part_far, grad_far = score(got[2], label_weights, label_count, block, [[0, 1, 2]], part_mid)
    back_far = exchange(part_far)
    weight_grad = weight_gradient(list(zip(got, [grad_own, grad_mid, grad_far])), width, block, per_dst)
    part_near, back_far, weight_grad = lax.optimization_barrier((part_near, back_far, weight_grad))
    back_near = exchange(part_near)

    order = [(0, i) for i in mid[2:]] + [(1, 0), (1, 1), (1, 2)]
    parts = [1] * (len(order) - 1) + [2]
    sums = list(combine(back_far, picks[1:], order, parts, width, (), PARAMS))
    to_lower, to_upper = down(sums[-2]), up(sums[-1])
    sums = sums[:-2]
    sums[-2:] = [add_half(sums[-2], to_lower, False), add_half(sums[-1], to_upper, True)]
    to_lower, to_upper = down(sums[-2]), up(sums[-1])
    sums = sums[:-2]
    while sums:
        to_lower, to_upper = down(add(sums[-2], to_lower)), up(add(sums[-1], to_upper))
        sums = sums[:-2]
    order = [(0, 0), (1, 0), (1, 1)]
    arrived = ((1, to_lower), (2, to_upper))
    mine, a, b = combine(back_near, picks[:2], order, [1, 1, 1], width, arrived)
    to_lower, to_upper = down(a), up(b)
    total = mine.astype(F32) + to_lower.astype(F32) + to_upper.astype(F32)
    enc_grad = total[:, 0:width].astype(BF16)
    query_loss = total[:, width] / (top * labels)
    return enc_grad, query_loss, weight_grad


def solution(mesh):
    in_specs = (
        P(("grp", "dev"), None),
        P(("grp", "dev"), None),
        P(("grp", "dev")),
        P(("grp", "dev"), None),
        P(("grp", "dev"), None),
    )
    out_specs = (P(("grp", "dev"), None), P(("grp", "dev")), P(("grp", "dev"), None))
    return jax.shard_map(
        per_device, mesh=mesh, in_specs=in_specs, out_specs=out_specs, check_vma=False
    )
```

time: 251 us -> 199 us (0.79)
  blocking collectives: 125 us -> 0 us
  starting transfers between devices: 0.08 us -> 62.9 us
  waiting for transfers between devices: 78 us -> 94.3 us
  between operations: 14 us -> 0.87 us
  Pallas kernels: 25.6 us -> 35.3 us
  other arithmetic: 4.47 us -> 1 us
    all_to_all x2 -> x0, blocking collectives: 125 us -> none  [the longest x1 63.1 us: per_device(): lax.all_to_all(send, 'dev', split_axis=0, concat_axis=0, tiled=True)]
    all_to_all x0 -> x5, waiting for transfers between devices: none -> 50 us  [exchange(): return lax.all_to_all(v, 'dev', split_axis=0, concat_axis=0, tiled=True)]
    all_gather x1 -> x0, waiting for transfers between devices: 44.6 us -> none  [per_device(): gathered = lax.all_gather(own, 'grp', axis=0, tiled=False)]
    ppermute x0 -> x16, waiting for transfers between devices: none -> 44.3 us  [the longest x8 26.3 us: down(): return lax.ppermute(v, 'grp', down_pairs)]
    all_to_all x0 -> x5, starting transfers between devices: none -> 34.5 us  [exchange(): return lax.all_to_all(v, 'dev', split_axis=0, concat_axis=0, tiled=True)]
    reduce_scatter x1 -> x0, waiting for transfers between devices: 33.4 us -> none  [per_device(): total = lax.psum_scatter(partial, 'grp', scatter_dimension=0, tiled=True)]
    ppermute x0 -> x16, starting transfers between devices: none -> 28.4 us  [the longest x8 25.8 us: down(): return lax.ppermute(v, 'grp', down_pairs)]
    pallas_call x4 -> x10, Pallas kernels: 25.6 us -> 35.3 us  [the longest x3 14.9 us: score(): pl.pallas_call(functools.partial(score_kernel, per_dst=per_dst, carried=c...]
  transfers between devices with their start and end apart: 2 -> 21, of which waited for: 2 -> 14; matrix products, arithmetic and copies ran while one was open for 0% -> 0% of each run, Pallas kernels for 3% -> 12%
where the time goes in v2:
time: 199 us; the launch traced here: 198 us
  waiting for transfers between devices  94.3 us (47%)
  starting transfers between devices  62.9 us (32%)
  Pallas kernels  35.3 us (18%)
  local copies, waits for them, and re-layouts  3.98 us (2%)
    all_to_all x5, waiting for transfers between devices, exchange(): return lax.all_to_all(v, 'dev', split_axis=0, concat_axis=0, tiled=True)  50 us
    all_to_all x5, starting transfers between devices, exchange(): return lax.all_to_all(v, 'dev', split_axis=0, concat_axis=0, tiled=True)  34.5 us
    ppermute x8, waiting for transfers between devices, down(): return lax.ppermute(v, 'grp', down_pairs)  26.3 us
    ppermute x8, starting transfers between devices, down(): return lax.ppermute(v, 'grp', down_pairs)  25.8 us
    ppermute x8, waiting for transfers between devices, up(): return lax.ppermute(v, 'grp', up_pairs)  18 us
    pallas_call x3, Pallas kernels, score(): pl.pallas_call(functools.partial(score_kernel, per_dst=per_dst, carried=c...  14.9 us
    pallas_call x3, Pallas kernels, dispatch(): pl.pallas_call(functools.partial(dispatch_kernel, parts=[len(blocks) for...  7.15 us
    pallas_call x1, Pallas kernels, weight_gradient(): pl.pallas_call(functools.partial(weight_kernel, per_dst=per_dst), grid=(d...  6.5 us
  transfers between devices with their start and end apart: 21, of which 14 were waited for; matrix products, arithmetic and copies ran while one was open for 0% of the time, Pallas kernels for 12%

profile of v2, /device:TPU:2, one launch (start us, length us, event | category | flops | bytes accessed | tf_op | source)
XLA Modules:
  0.0 198.4 jit_solution(14341338538332633958)
XLA Ops:
  2.4 5.9 %collective-permute-start.3 = (bf16[144,1024]{1,0:T(8,128)(2,1)}, bf16[144,1024]{1,0:T(8,128)(2,1)S(1)}, u32[]{:S(2)}, u32[]{:S(2)}) collective-permute-start(bf16[144,1024]{1,0:T(8,128)(2,1)} %prepare.1.refs_0_), channel_id=1, source_target_pairs={{0,224},{32,0},{64,32},{96,64},{128,96},{160,128},{192,160},{224,1... | collective-permute-start | bytes 884744 | tf_op jit(solution)/shard_map/ppermute | solution.py:413
  10.9 7.6 %all-to-all-start = ((bf16[32,72,128]{2,1,0:T(8,128)(2,1)}), bf16[32,72,128]{2,1,0:T(8,128)(2,1)S(1)}, u32[]{:S(2)}, u32[]{:S(2)}) async-start(bf16[32,72,128]{2,1,0:T(8,128)(2,1)} %get-tuple-element.36), calls=%async_computation | async-start | bytes 1179648 | tf_op jit(solution)/shard_map/all_to_all | solution.py:416
  18.5 3.3 %collective-permute-start.4 = (bf16[144,1024]{1,0:T(8,128)(2,1)S(1)}, bf16[144,1024]{1,0:T(8,128)(2,1)S(1)}, u32[]{:S(2)}, u32[]{:S(2)}) collective-permute-start(bf16[144,1024]{1,0:T(8,128)(2,1)S(1)} %collective-permute-done.3.refs_1_), channel_id=1, source_target_pairs={{0,224},{32,0},{64,32},{96,64},{128,96},{160,128},{192,160},{224,1... | collective-permute-start | bytes 884744 | tf_op jit(solution)/shard_map/ppermute | solution.py:413
  21.8 6.6 %collective-permute-done.4.refs_3_ = bf16[144,1024]{1,0:T(8,128)(2,1)S(1)} collective-permute-done((bf16[144,1024]{1,0:T(8,128)(2,1)S(1)}, bf16[144,1024]{1,0:T(8,128)(2,1)S(1)}, u32[]{:S(2)}, u32[]{:S(2)}) %collective-permute-start.4) | collective-permute-done | bytes 294944 | tf_op jit(solution)/shard_map/ppermute | solution.py:413
  28.4 3.4 %collective-permute-done.1.refs_2_ = bf16[144,1024]{1,0:T(8,128)(2,1)S(1)} collective-permute-done((bf16[144,1024]{1,0:T(8,128)(2,1)S(1)}, bf16[144,1024]{1,0:T(8,128)(2,1)S(1)}, u32[]{:S(2)}, u32[]{:S(2)}) %collective-permute-start.1) | collective-permute-done | bytes 294944 | tf_op jit(solution)/shard_map/ppermute | solution.py:410
  31.8 3.1 %dispatch.4 = (bf16[32,264,128]{2,1,0:T(8,128)(2,1)}, bf16[4,256,128]{2,1,0:T(8,128)(2,1)S(1)}) custom-call(s32[1]{0:T(128)} %bitcast.grp_ref, bf16[144,1024]{1,0:T(8,128)(2,1)S(1)} %collective-permute-done.refs_0_, bf16[144,1024]{1,0:T(8,128)(2,1)S(1)} %collective-permute-done.3.refs_1_, bf16[144,1024]{1,0:T(8,128)(2,1)S(1)} %collective-permute-done.1.refs_2_, ...), custom_call_target="tpu_custom_call" | custom-call | tf_op jit(solution)/shard_map/dispatch/pallas_call | solution.py:150
  36.4 7.4 %all-to-all-start.1 = ((bf16[32,264,128]{2,1,0:T(8,128)(2,1)}), bf16[32,264,128]{2,1,0:T(8,128)(2,1)}, u32[]{:S(2)}, u32[]{:S(2)}) async-start(bf16[32,264,128]{2,1,0:T(8,128)(2,1)} %get-tuple-element.37), calls=%async_computation.1 | async-start | bytes 4325376 | tf_op jit(solution)/shard_map/all_to_all | solution.py:416
  45.9 7.0 %collective-permute-done.5.refs_1_ = bf16[144,1024]{1,0:T(8,128)(2,1)S(1)} collective-permute-done((bf16[144,1024]{1,0:T(8,128)(2,1)S(1)}, bf16[144,1024]{1,0:T(8,128)(2,1)S(1)}, u32[]{:S(2)}, u32[]{:S(2)}) %collective-permute-start.5) | collective-permute-done | bytes 294944 | tf_op jit(solution)/shard_map/ppermute | solution.py:413
  55.2 5.6 %collective-permute-done.6.refs_2_ = bf16[64,1024]{1,0:T(8,128)(2,1)S(1)} collective-permute-done((bf16[64,1024]{1,0:T(8,128)(2,1)S(1)}, bf16[64,1024]{1,0:T(8,128)(2,1)S(1)}, u32[]{:S(2)}, u32[]{:S(2)}) %collective-permute-start.6) | collective-permute-done | bytes 131104 | tf_op jit(solution)/shard_map/ppermute | solution.py:410
  60.8 2.5 %dispatch.3 = (bf16[32,200,128]{2,1,0:T(8,128)(2,1)}, bf16[3,256,128]{2,1,0:T(8,128)(2,1)S(1)}) custom-call(s32[1]{0:T(128)} %bitcast.grp_ref, bf16[144,1024]{1,0:T(8,128)(2,1)S(1)} %collective-permute-done.2.refs_0_, bf16[144,1024]{1,0:T(8,128)(2,1)S(1)} %collective-permute-done.5.refs_1_, bf16[64,1024]{1,0:T(8,128)(2,1)S(1)} %collective-permute-done.6.refs_2_, ...), custom_call_target="tpu_custom_call" | custom-call | tf_op jit(solution)/shard_map/dispatch/pallas_call | solution.py:150
  64.0 8.4 %all-to-all-done.1.x_ref.refs_2_ = bf16[32,264,128]{2,1,0:T(8,128)(2,1)} async-done(((bf16[32,264,128]{2,1,0:T(8,128)(2,1)}), bf16[32,264,128]{2,1,0:T(8,128)(2,1)}, u32[]{:S(2)}, u32[]{:S(2)}) %all-to-all-start.1) | async-done | bytes 2162720 | tf_op jit(solution)/shard_map/all_to_all | solution.py:416
  72.5 6.7 %all-to-all-start.2 = ((bf16[32,200,128]{2,1,0:T(8,128)(2,1)}), bf16[32,200,128]{2,1,0:T(8,128)(2,1)}, u32[]{:S(2)}, u32[]{:S(2)}) async-start(bf16[32,200,128]{2,1,0:T(8,128)(2,1)} %get-tuple-element.44), calls=%async_computation.2 | async-start | bytes 3276800 | tf_op jit(solution)/shard_map/all_to_all | solution.py:416
  79.1 3.7 %score.3 = (bf16[32,72,128]{2,1,0:T(8,128)(2,1)}, bf16[256,128]{1,0:T(8,128)(2,1)}) custom-call(s32[4]{0:T(128)} %count_ref.5, bf16[32,72,128]{2,1,0:T(8,128)(2,1)} %copy-done.4, bf16[512,1024]{1,0:T(8,128)(2,1)} %w_ref.5), custom_call_target="tpu_custom_call" | custom-call | flops 536870912 | bytes 2228224 | tf_op jit(solution)/shard_map/score/pallas_call | solution.py:246
  82.9 5.9 %score.4 = (bf16[32,200,128]{2,1,0:T(8,128)(2,1)}, bf16[32,136,128]{2,1,0:T(8,128)(2,1)}, bf16[1024,128]{1,0:T(8,128)(2,1)}) custom-call(s32[4]{0:T(128)} %count_ref.5, bf16[32,264,128]{2,1,0:T(8,128)(2,1)} %all-to-all-done.1.x_ref.refs_2_, bf16[512,1024]{1,0:T(8,128)(2,1)} %w_ref.5, bf16[32,72,128]{2,1,0:T(8,128)(2,1)} %get-tuple-element.40.refs_0_), custom_call_target="tpu_custom_call" | custom-call | flops 2147483648 | bytes 5767168 | tf_op jit(solution)/shard_map/score/pallas_call | solution.py:246
  88.7 13.3 %all-to-all-done.2.x_ref.refs_4_ = bf16[32,200,128]{2,1,0:T(8,128)(2,1)} async-done(((bf16[32,200,128]{2,1,0:T(8,128)(2,1)}), bf16[32,200,128]{2,1,0:T(8,128)(2,1)}, u32[]{:S(2)}, u32[]{:S(2)}) %all-to-all-start.2) | async-done | bytes 1638432 | tf_op jit(solution)/shard_map/all_to_all | solution.py:416
  102.1 5.3 %score.5 = (bf16[32,328,128]{2,1,0:T(8,128)(2,1)}, bf16[768,128]{1,0:T(8,128)(2,1)}) custom-call(s32[4]{0:T(128)} %count_ref.5, bf16[32,200,128]{2,1,0:T(8,128)(2,1)} %all-to-all-done.2.x_ref.refs_4_, bf16[512,1024]{1,0:T(8,128)(2,1)} %w_ref.5, bf16[32,136,128]{2,1,0:T(8,128)(2,1)} %get-tuple-element.45.refs_0_), custom_call_target="tpu_custom_call" | custom-call | flops 1610612736 | bytes 4587520 | tf_op jit(solution)/shard_map/score/pallas_call | solution.py:246
  107.4 6.5 %all-to-all-start.3 = ((bf16[32,328,128]{2,1,0:T(8,128)(2,1)}), bf16[32,328,128]{2,1,0:T(8,128)(2,1)}, u32[]{:S(2)}, u32[]{:S(2)}) async-start(bf16[32,328,128]{2,1,0:T(8,128)(2,1)} %get-tuple-element.46), calls=%async_computation.3 | async-start | bytes 5373952 | tf_op jit(solution)/shard_map/all_to_all | solution.py:416
  113.9 6.5 %weight_gradient.1 = f32[512,1024]{1,0:T(8,128)} custom-call(bf16[32,72,128]{2,1,0:T(8,128)(2,1)} %copy-done.4, bf16[256,128]{1,0:T(8,128)(2,1)} %get-tuple-element.47.refs_1_, bf16[32,264,128]{2,1,0:T(8,128)(2,1)} %all-to-all-done.1.x_ref.refs_2_, bf16[1024,128]{1,0:T(8,128)(2,1)} %get-tuple-element.48.refs_3_, ...), custom_call_target="tpu_custom_call" | custom-call | flops 2147483648 | bytes 8388608 | tf_op jit(solution)/shard_map/weight_gradient/pallas_call | solution.py:303
  120.4 28.2 %all-to-all-done.3.ret_ref = bf16[32,328,128]{2,1,0:T(8,128)(2,1)} async-done(((bf16[32,328,128]{2,1,0:T(8,128)(2,1)}), bf16[32,328,128]{2,1,0:T(8,128)(2,1)}, u32[]{:S(2)}, u32[]{:S(2)}) %all-to-all-start.3) | async-done | bytes 2687008 | tf_op jit(solution)/shard_map/all_to_all | solution.py:416
  148.6 3.8 %combine.2 = (bf16[128,1152]{1,0:T(8,128)(2,1)}, bf16[128,1152]{1,0:T(8,128)(2,1)}, bf16[128,1152]{1,0:T(8,128)(2,1)}, bf16[128,1152]{1,0:T(8,128)(2,1)}, bf16[6...) custom-call(bf16[32,328,128]{2,1,0:T(8,128)(2,1)} %all-to-all-done.3.ret_ref, bf16[4,256,128]{2,1,0:T(8,128)(2,1)} %copy-done.1, ...), custom_call_target="tpu_custom_call" | custom-call | tf_op jit(solution)/shard_map/combine/pallas_call | solution.py:367
  152.6 6.2 %all-to-all-start.4 = ((bf16[32,200,128]{2,1,0:T(8,128)(2,1)}), bf16[32,200,128]{2,1,0:T(8,128)(2,1)S(1)}, u32[]{:S(2)}, u32[]{:S(2)}) async-start(bf16[32,200,128]{2,1,0:T(8,128)(2,1)} %get-tuple-element.50), calls=%async_computation.4 | async-start | bytes 3276800 | tf_op jit(solution)/shard_map/all_to_all | solution.py:416
  158.8 3.2 %collective-permute-start.8 = (bf16[64,1152]{1,0:T(8,128)(2,1)S(1)}, bf16[64,1152]{1,0:T(8,128)(2,1)S(1)}, u32[]{:S(2)}, u32[]{:S(2)}) collective-permute-start(bf16[64,1152]{1,0:T(8,128)(2,1)S(1)} %copy-done.9), channel_id=1, source_target_pairs={{0,224},{32,0},{64,32},{96,64},{128,96},{160,128},{192,160},{224,1... | collective-permute-start | bytes 442376 | tf_op jit(solution)/shard_map/ppermute | solution.py:413
  162.1 3.3 %collective-permute-done.8 = bf16[64,1152]{1,0:T(8,128)(2,1)S(1)} collective-permute-done((bf16[64,1152]{1,0:T(8,128)(2,1)S(1)}, bf16[64,1152]{1,0:T(8,128)(2,1)S(1)}, u32[]{:S(2)}, u32[]{:S(2)}) %collective-permute-start.8) | collective-permute-done | bytes 147488 | tf_op jit(solution)/shard_map/ppermute | solution.py:413
  165.5 3.8 %collective-permute-start.9 = (bf16[128,1152]{1,0:T(8,128)(2,1)S(1)}, bf16[128,1152]{1,0:T(8,128)(2,1)S(1)}, u32[]{:S(2)}, u32[]{:S(2)}) collective-permute-start(bf16[128,1152]{1,0:T(8,128)(2,1)S(1)} %add_convert_fusion.3), channel_id=1, source_target_pairs={{0,224},{32,0},{64,32},{96,64},{128,96},{160,128},{192,160},{224,1... | collective-permute-start | bytes 884744 | tf_op jit(solution)/shard_map/ppermute | solution.py:413
  169.2 2.9 %collective-permute-done.12 = bf16[128,1152]{1,0:T(8,128)(2,1)S(1)} collective-permute-done((bf16[128,1152]{1,0:T(8,128)(2,1)S(1)}, bf16[128,1152]{1,0:T(8,128)(2,1)S(1)}, u32[]{:S(2)}, u32[]{:S(2)}) %collective-permute-start.12) | collective-permute-done | bytes 294944 | tf_op jit(solution)/shard_map/ppermute | solution.py:410
  172.3 2.7 %collective-permute-done.9 = bf16[128,1152]{1,0:T(8,128)(2,1)S(1)} collective-permute-done((bf16[128,1152]{1,0:T(8,128)(2,1)S(1)}, bf16[128,1152]{1,0:T(8,128)(2,1)S(1)}, u32[]{:S(2)}, u32[]{:S(2)}) %collective-permute-start.9) | collective-permute-done | bytes 294944 | tf_op jit(solution)/shard_map/ppermute | solution.py:413
  175.1 4.0 %collective-permute-start.10 = (bf16[128,1152]{1,0:T(8,128)(2,1)S(1)}, bf16[128,1152]{1,0:T(8,128)(2,1)S(1)}, u32[]{:S(2)}, u32[]{:S(2)}) collective-permute-start(bf16[128,1152]{1,0:T(8,128)(2,1)S(1)} %add_convert_fusion.2), channel_id=1, source_target_pairs={{0,224},{32,0},{64,32},{96,64},{128,96},{160,128},{192,160},{224,1... | collective-permute-start | bytes 884744 | tf_op jit(solution)/shard_map/ppermute | solution.py:413
  179.1 2.3 %collective-permute-done.13.refs_3_ = bf16[128,1152]{1,0:T(8,128)(2,1)S(1)} collective-permute-done((bf16[128,1152]{1,0:T(8,128)(2,1)S(1)}, bf16[128,1152]{1,0:T(8,128)(2,1)S(1)}, u32[]{:S(2)}, u32[]{:S(2)}) %collective-permute-start.13) | collective-permute-done | bytes 294944 | tf_op jit(solution)/shard_map/ppermute | solution.py:410
  181.4 2.5 %collective-permute-done.10.refs_2_ = bf16[128,1152]{1,0:T(8,128)(2,1)S(1)} collective-permute-done((bf16[128,1152]{1,0:T(8,128)(2,1)S(1)}, bf16[128,1152]{1,0:T(8,128)(2,1)S(1)}, u32[]{:S(2)}, u32[]{:S(2)}) %collective-permute-start.10) | collective-permute-done | bytes 294944 | tf_op jit(solution)/shard_map/ppermute | solution.py:413
  185.2 3.8 %collective-permute-start.14 = (bf16[128,1152]{1,0:T(8,128)(2,1)S(1)}, bf16[128,1152]{1,0:T(8,128)(2,1)S(1)}, u32[]{:S(2)}, u32[]{:S(2)}) collective-permute-start(bf16[128,1152]{1,0:T(8,128)(2,1)S(1)} %get-tuple-element.62), channel_id=1, source_target_pairs={{0,224},{32,0},{64,32},{96,64},{128,96},{160,128},{192,160},{224,1... | collective-permute-start | bytes 884744 | tf_op jit(solution)/shard_map/ppermute | solution.py:413
  189.0 4.2 %collective-permute-done.14 = bf16[128,1152]{1,0:T(8,128)(2,1)S(1)} collective-permute-done((bf16[128,1152]{1,0:T(8,128)(2,1)S(1)}, bf16[128,1152]{1,0:T(8,128)(2,1)S(1)}, u32[]{:S(2)}, u32[]{:S(2)}) %collective-permute-start.14) | collective-permute-done | bytes 294944 | tf_op jit(solution)/shard_map/ppermute | solution.py:413
  193.2 3.7 %collective-permute-done.15 = bf16[128,1152]{1,0:T(8,128)(2,1)S(1)} collective-permute-done((bf16[128,1152]{1,0:T(8,128)(2,1)S(1)}, bf16[128,1152]{1,0:T(8,128)(2,1)S(1)}, u32[]{:S(2)}, u32[]{:S(2)}) %collective-permute-start.15) | collective-permute-done | bytes 294944 | tf_op jit(solution)/shard_map/ppermute | solution.py:410
  (49 shorter events, 14.1 us)
Async XLA Ops:
  2.4 16.1 %collective-permute-start.3 = (bf16[144,1024]{1,0:T(8,128)(2,1)}, bf16[144,1024]{1,0:T(8,128)(2,1)S(1)}, u32[]{:S(2)}, u32[]{:S(2)}) collective-permute-start(bf16[144,1024]{1,0:T(8,128)(2,1)} %prepare.1.refs_0_), channel_id=1, source_target_pairs={{0,224},{32,0},{64,32},{96,64},{128,96},{160,128},{192,160},{224,1... | collective-permute-start | bytes 884744 | tf_op jit(solution)/shard_map/ppermute | solution.py:413
  8.3 13.5 %collective-permute-start = (bf16[144,1024]{1,0:T(8,128)(2,1)}, bf16[144,1024]{1,0:T(8,128)(2,1)S(1)}, u32[]{:S(2)}, u32[]{:S(2)}) collective-permute-start(bf16[144,1024]{1,0:T(8,128)(2,1)} %prepare.1.refs_0_), channel_id=1, source_target_pairs={{0,32},{32,64},{64,96},{96,128},{128,160},{160,192},{192,224},{224... | collective-permute-start | bytes 884744 | tf_op jit(solution)/shard_map/ppermute | solution.py:410
  8.3 1.0 copy-start
  10.9 24.7 %all-to-all-start = ((bf16[32,72,128]{2,1,0:T(8,128)(2,1)}), bf16[32,72,128]{2,1,0:T(8,128)(2,1)S(1)}, u32[]{:S(2)}, u32[]{:S(2)}) async-start(bf16[32,72,128]{2,1,0:T(8,128)(2,1)} %get-tuple-element.36), calls=%async_computation | async-start | bytes 1179648 | tf_op jit(solution)/shard_map/all_to_all | solution.py:416
  18.5 9.9 %collective-permute-start.4 = (bf16[144,1024]{1,0:T(8,128)(2,1)S(1)}, bf16[144,1024]{1,0:T(8,128)(2,1)S(1)}, u32[]{:S(2)}, u32[]{:S(2)}) collective-permute-start(bf16[144,1024]{1,0:T(8,128)(2,1)S(1)} %collective-permute-done.3.refs_1_), channel_id=1, source_target_pairs={{0,224},{32,0},{64,32},{96,64},{128,96},{160,128},{192,160},{224,1... | collective-permute-start | bytes 884744 | tf_op jit(solution)/shard_map/ppermute | solution.py:413
  21.8 10.0 %collective-permute-start.1 = (bf16[144,1024]{1,0:T(8,128)(2,1)S(1)}, bf16[144,1024]{1,0:T(8,128)(2,1)S(1)}, u32[]{:S(2)}, u32[]{:S(2)}) collective-permute-start(bf16[144,1024]{1,0:T(8,128)(2,1)S(1)} %collective-permute-done.refs_0_), channel_id=1, source_target_pairs={{0,32},{32,64},{64,96},{96,128},{128,160},{160,192},{192,224},{224... | collective-permute-start | bytes 884744 | tf_op jit(solution)/shard_map/ppermute | solution.py:410
  34.9 0.7 copy-start.1
  35.6 0.8 copy-start.4
  36.4 36.1 %all-to-all-start.1 = ((bf16[32,264,128]{2,1,0:T(8,128)(2,1)}), bf16[32,264,128]{2,1,0:T(8,128)(2,1)}, u32[]{:S(2)}, u32[]{:S(2)}) async-start(bf16[32,264,128]{2,1,0:T(8,128)(2,1)} %get-tuple-element.37), calls=%async_computation.1 | async-start | bytes 4325376 | tf_op jit(solution)/shard_map/all_to_all | solution.py:416
  43.8 9.1 %collective-permute-start.5 = (bf16[144,1024]{1,0:T(8,128)(2,1)S(1)}, bf16[144,1024]{1,0:T(8,128)(2,1)S(1)}, u32[]{:S(2)}, u32[]{:S(2)}) collective-permute-start(bf16[144,1024]{1,0:T(8,128)(2,1)S(1)} %collective-permute-done.4.refs_3_), channel_id=1, source_target_pairs={{0,224},{32,0},{64,32},{96,64},{128,96},{160,128},{192,160},{224,1... | collective-permute-start | bytes 884744 | tf_op jit(solution)/shard_map/ppermute | solution.py:413
  44.2 10.4 %collective-permute-start.2 = (bf16[144,1024]{1,0:T(8,128)(2,1)S(1)}, bf16[144,1024]{1,0:T(8,128)(2,1)S(1)}, u32[]{:S(2)}, u32[]{:S(2)}) collective-permute-start(bf16[144,1024]{1,0:T(8,128)(2,1)S(1)} %collective-permute-done.1.refs_2_), channel_id=1, source_target_pairs={{0,32},{32,64},{64,96},{96,128},{128,160},{160,192},{192,224},{224... | collective-permute-start | bytes 884744 | tf_op jit(solution)/shard_map/ppermute | solution.py:410
  53.0 7.8 %collective-permute-start.7 = (bf16[80,1024]{1,0:T(8,128)(2,1)S(1)}, bf16[80,1024]{1,0:T(8,128)(2,1)S(1)}, u32[]{:S(2)}, u32[]{:S(2)}) collective-permute-start(bf16[80,1024]{1,0:T(8,128)(2,1)S(1)} %slice.18), channel_id=1, source_target_pairs={{0,224},{32,0},{64,32},{96,64},{128,96},{160,128},{192,160},{224,1... | collective-permute-start | bytes 491528 | tf_op jit(solution)/shard_map/ppermute | solution.py:413
  54.5 6.3 %collective-permute-start.6 = (bf16[64,1024]{1,0:T(8,128)(2,1)S(1)}, bf16[64,1024]{1,0:T(8,128)(2,1)S(1)}, u32[]{:S(2)}, u32[]{:S(2)}) collective-permute-start(bf16[64,1024]{1,0:T(8,128)(2,1)S(1)} %slice.17), channel_id=1, source_target_pairs={{0,32},{32,64},{64,96},{96,128},{128,160},{160,192},{192,224},{224... | collective-permute-start | bytes 393224 | tf_op jit(solution)/shard_map/ppermute | solution.py:410
  63.4 0.7 copy-start.3
  72.5 29.6 %all-to-all-start.2 = ((bf16[32,200,128]{2,1,0:T(8,128)(2,1)}), bf16[32,200,128]{2,1,0:T(8,128)(2,1)}, u32[]{:S(2)}, u32[]{:S(2)}) async-start(bf16[32,200,128]{2,1,0:T(8,128)(2,1)} %get-tuple-element.44), calls=%async_computation.2 | async-start | bytes 3276800 | tf_op jit(solution)/shard_map/all_to_all | solution.py:416
  107.4 41.2 %all-to-all-start.3 = ((bf16[32,328,128]{2,1,0:T(8,128)(2,1)}), bf16[32,328,128]{2,1,0:T(8,128)(2,1)}, u32[]{:S(2)}, u32[]{:S(2)}) async-start(bf16[32,328,128]{2,1,0:T(8,128)(2,1)} %get-tuple-element.46), calls=%async_computation.3 | async-start | bytes 5373952 | tf_op jit(solution)/shard_map/all_to_all | solution.py:416
  152.4 6.4 %copy-start.9 = (bf16[64,1152]{1,0:T(8,128)(2,1)S(1)}, bf16[64,1152]{1,0:T(8,128)(2,1)}, u32[]{:S(2)}) copy-start(bf16[64,1152]{1,0:T(8,128)(2,1)} %get-tuple-element.57) | copy-start | bytes 442372
  152.4 9.6 %copy-start.8 = (bf16[128,1152]{1,0:T(8,128)(2,1)S(1)}, bf16[128,1152]{1,0:T(8,128)(2,1)}, u32[]{:S(2)}) copy-start(bf16[128,1152]{1,0:T(8,128)(2,1)} %get-tuple-element.59) | copy-start | bytes 884740
  152.4 13.0 %copy-start.7 = (bf16[128,1152]{1,0:T(8,128)(2,1)S(1)}, bf16[128,1152]{1,0:T(8,128)(2,1)}, u32[]{:S(2)}) copy-start(bf16[128,1152]{1,0:T(8,128)(2,1)} %get-tuple-element.56) | copy-start | bytes 884740
  152.4 19.7 %copy-start.6 = (bf16[128,1152]{1,0:T(8,128)(2,1)S(1)}, bf16[128,1152]{1,0:T(8,128)(2,1)}, u32[]{:S(2)}) copy-start(bf16[128,1152]{1,0:T(8,128)(2,1)} %get-tuple-element.58) | copy-start | bytes 884740
  152.5 22.5 %copy-start.5 = (bf16[128,1152]{1,0:T(8,128)(2,1)S(1)}, bf16[128,1152]{1,0:T(8,128)(2,1)}, u32[]{:S(2)}) copy-start(bf16[128,1152]{1,0:T(8,128)(2,1)} %get-tuple-element.55) | copy-start | bytes 884740
  152.5 9.5 %collective-permute-start.11 = (bf16[64,1152]{1,0:T(8,128)(2,1)}, bf16[64,1152]{1,0:T(8,128)(2,1)S(1)}, u32[]{:S(2)}, u32[]{:S(2)}) collective-permute-start(bf16[64,1152]{1,0:T(8,128)(2,1)} %get-tuple-element.60), channel_id=1, source_target_pairs={{0,32},{32,64},{64,96},{96,128},{128,160},{160,192},{192,224},{224... | collective-permute-start | bytes 442376 | tf_op jit(solution)/shard_map/ppermute | solution.py:410
  152.6 31.3 %all-to-all-start.4 = ((bf16[32,200,128]{2,1,0:T(8,128)(2,1)}), bf16[32,200,128]{2,1,0:T(8,128)(2,1)S(1)}, u32[]{:S(2)}, u32[]{:S(2)}) async-start(bf16[32,200,128]{2,1,0:T(8,128)(2,1)} %get-tuple-element.50), calls=%async_computation.4 | async-start | bytes 3276800 | tf_op jit(solution)/shard_map/all_to_all | solution.py:416
  158.8 25.1 %copy-start.2 = (bf16[4,256,128]{2,1,0:T(8,128)(2,1)S(1)}, bf16[4,256,128]{2,1,0:T(8,128)(2,1)}, u32[]{:S(2)}) copy-start(bf16[4,256,128]{2,1,0:T(8,128)(2,1)} %copy-done.1) | copy-start | bytes 786436
  158.8 6.6 %collective-permute-start.8 = (bf16[64,1152]{1,0:T(8,128)(2,1)S(1)}, bf16[64,1152]{1,0:T(8,128)(2,1)S(1)}, u32[]{:S(2)}, u32[]{:S(2)}) collective-permute-start(bf16[64,1152]{1,0:T(8,128)(2,1)S(1)} %copy-done.9), channel_id=1, source_target_pairs={{0,224},{32,0},{64,32},{96,64},{128,96},{160,128},{192,160},{224,1... | collective-permute-start | bytes 442376 | tf_op jit(solution)/shard_map/ppermute | solution.py:413
  162.0 10.1 %collective-permute-start.12 = (bf16[128,1152]{1,0:T(8,128)(2,1)S(1)}, bf16[128,1152]{1,0:T(8,128)(2,1)S(1)}, u32[]{:S(2)}, u32[]{:S(2)}) collective-permute-start(bf16[128,1152]{1,0:T(8,128)(2,1)S(1)} %add_convert_fusion.1), channel_id=1, source_target_pairs={{0,32},{32,64},{64,96},{96,128},{128,160},{160,192},{192,224},{224... | collective-permute-start | bytes 884744 | tf_op jit(solution)/shard_map/ppermute | solution.py:410
  165.5 9.5 %collective-permute-start.9 = (bf16[128,1152]{1,0:T(8,128)(2,1)S(1)}, bf16[128,1152]{1,0:T(8,128)(2,1)S(1)}, u32[]{:S(2)}, u32[]{:S(2)}) collective-permute-start(bf16[128,1152]{1,0:T(8,128)(2,1)S(1)} %add_convert_fusion.3), channel_id=1, source_target_pairs={{0,224},{32,0},{64,32},{96,64},{128,96},{160,128},{192,160},{224,1... | collective-permute-start | bytes 884744 | tf_op jit(solution)/shard_map/ppermute | solution.py:413
  172.2 9.2 %collective-permute-start.13 = (bf16[128,1152]{1,0:T(8,128)(2,1)S(1)}, bf16[128,1152]{1,0:T(8,128)(2,1)S(1)}, u32[]{:S(2)}, u32[]{:S(2)}) collective-permute-start(bf16[128,1152]{1,0:T(8,128)(2,1)S(1)} %add_convert_fusion), channel_id=1, source_target_pairs={{0,32},{32,64},{64,96},{96,128},{128,160},{160,192},{192,224},{224... | collective-permute-start | bytes 884744 | tf_op jit(solution)/shard_map/ppermute | solution.py:410
  175.1 8.8 %collective-permute-start.10 = (bf16[128,1152]{1,0:T(8,128)(2,1)S(1)}, bf16[128,1152]{1,0:T(8,128)(2,1)S(1)}, u32[]{:S(2)}, u32[]{:S(2)}) collective-permute-start(bf16[128,1152]{1,0:T(8,128)(2,1)S(1)} %add_convert_fusion.2), channel_id=1, source_target_pairs={{0,224},{32,0},{64,32},{96,64},{128,96},{160,128},{192,160},{224,1... | collective-permute-start | bytes 884744 | tf_op jit(solution)/shard_map/ppermute | solution.py:413
  185.2 8.0 %collective-permute-start.14 = (bf16[128,1152]{1,0:T(8,128)(2,1)S(1)}, bf16[128,1152]{1,0:T(8,128)(2,1)S(1)}, u32[]{:S(2)}, u32[]{:S(2)}) collective-permute-start(bf16[128,1152]{1,0:T(8,128)(2,1)S(1)} %get-tuple-element.62), channel_id=1, source_target_pairs={{0,224},{32,0},{64,32},{96,64},{128,96},{160,128},{192,160},{224,1... | collective-permute-start | bytes 884744 | tf_op jit(solution)/shard_map/ppermute | solution.py:413
  189.0 7.9 %collective-permute-start.15 = (bf16[128,1152]{1,0:T(8,128)(2,1)S(1)}, bf16[128,1152]{1,0:T(8,128)(2,1)S(1)}, u32[]{:S(2)}, u32[]{:S(2)}) collective-permute-start(bf16[128,1152]{1,0:T(8,128)(2,1)S(1)} %get-tuple-element.63), channel_id=1, source_target_pairs={{0,32},{32,64},{64,96},{96,128},{128,160},{160,192},{192,224},{224... | collective-permute-start | bytes 884744 | tf_op jit(solution)/shard_map/ppermute | solution.py:410

commit v3 on v2

--- a/solution.py
+++ b/solution.py
@@ -70,7 +70,8 @@
     parts = (group, matched - group * in_group, held[1])
     meta = jnp.concatenate([part.astype(F32) for part in parts], axis=1)
     meta = jnp.concatenate([meta, jnp.zeros((top, out_ref.shape[1] - meta.shape[1]), F32)], axis=1)
-    meta = jnp.concatenate([meta, jnp.zeros((META - top, meta.shape[1]), F32)], axis=0)
+    if META > top:
+        meta = jnp.concatenate([meta, jnp.zeros((META - top, meta.shape[1]), F32)], axis=0)
     out_ref[queries:] = meta.astype(BF16)
     copies[2].wait()
 
@@ -230,7 +231,7 @@
     return (x.shape[1] // TILE - 1) * LANES // width
 
 
-def score(x, weights, count, block, outs, carry=None):
+def score(x, weights, count, block, outs, carry=None, params=PARAMS):
     devs, tile_rows, _ = x.shape
     per_dst = count.shape[0]
     all_labels, width = weights.shape
@@ -256,7 +257,7 @@
         + ([by_dev(carry.shape[1])] if carried else []),
         out_specs=[by_dev(r) for r in ret_rows]
         + [pl.BlockSpec((block * slots, labels), lambda i: (i, 0))],
-        compiler_params=PARAMS,
+        compiler_params=params,
         cost_estimate=pl.CostEstimate(
             flops=4 * devs * slots * all_labels * width,
             bytes_accessed=4 * devs * slots * (width + labels) + 2 * all_labels * width,
@@ -363,7 +364,7 @@
     queries = picks[0].shape[2]
     shapes = [(queries // count, width + LANES) for count in parts for _ in range(count)]
     added = [a for _, a in arrived]
-    steps = 2
+    steps = 1
     return pl.pallas_call(
         functools.partial(
             combine_kernel,
@@ -394,6 +395,40 @@
     return add(a, jnp.concatenate([zero, half] if second else [half, zero], axis=0))
 
 
+def finish_kernel(mine_ref, lower_ref, upper_ref, grad_ref, loss_ref, grad, loss, sems, *, scale):
+    width = grad_ref.shape[1]
+    total = mine_ref[...].astype(F32) + lower_ref[...].astype(F32) + upper_ref[...].astype(F32)
+    grad[...] = total[:, 0:width].astype(BF16)
+    grad_copy = pltpu.make_async_copy(grad, grad_ref, sems.at[0])
+    grad_copy.start()
+    loss[...] = total[:, width:].T[0:1] * scale
+    loss_copy = pltpu.make_async_copy(loss, loss_ref, sems.at[1])
+    loss_copy.start()
+    grad_copy.wait()
+    loss_copy.wait()
+
+
+def finish(mine, to_lower, to_upper, scale):
+    queries, wide = mine.shape
+    width = wide - LANES
+    return pl.pallas_call(
+        functools.partial(finish_kernel, scale=scale),
+        out_shape=(
+            jax.ShapeDtypeStruct((queries, width), BF16),
+            jax.ShapeDtypeStruct((1, queries), F32),
+        ),
+        in_specs=[IN_VMEM] * 3,
+        out_specs=[IN_HBM] * 2,
+        scratch_shapes=[
+            pltpu.VMEM((queries, width), BF16),
+            pltpu.VMEM((1, queries), F32),
+            pltpu.SemaphoreType.DMA((2,)),
+        ],
+        compiler_params=SMALL,
+        name="finish",
+    )(mine, to_lower, to_upper)
+
+
 def per_device(encodings, label_weights, label_count, matched, positive):
     queries, width = encodings.shape
     top = matched.shape[1]
@@ -437,7 +472,7 @@
 
     block = min(16, dsts)
     mid = list(range(len(chunks[1])))
-    part_own, grad_own = score(got[0], label_weights, label_count, block, [[0]])
+    part_own, grad_own = score(got[0], label_weights, label_count, block, [[0]], None, SMALL)
     part_near, part_mid, grad_mid = score(
         got[1], label_weights, label_count, block, [mid[:2], mid[2:]], part_own
     )
@@ -463,9 +498,8 @@
     arrived = ((1, to_lower), (2, to_upper))
     mine, a, b = combine(back_near, picks[:2], order, [1, 1, 1], width, arrived)
     to_lower, to_upper = down(a), up(b)
-    total = mine.astype(F32) + to_lower.astype(F32) + to_upper.astype(F32)
-    enc_grad = total[:, 0:width].astype(BF16)
-    query_loss = total[:, width] / (top * labels)
+    enc_grad, query_loss = finish(mine, to_lower, to_upper, 1.0 / (top * labels))
+    query_loss = query_loss.reshape(queries)
     return enc_grad, query_loss, weight_grad
 
 

time: 199 us -> 197 us (0.990)
  transfers between devices with their start and end apart: 21 -> 21, of which waited for: 14 -> 14; matrix products, arithmetic and copies ran while one was open for 0% -> 0% of each run, Pallas kernels for 12% -> 11%
where the time goes in v3:
time: 197 us; the launch traced here: 196 us
  waiting for transfers between devices  94.4 us (48%)
  starting transfers between devices  62.7 us (32%)
  Pallas kernels  33.9 us (17%)
  local copies, waits for them, and re-layouts  3.88 us (2%)
    all_to_all x5, waiting for transfers between devices, exchange(): return lax.all_to_all(v, 'dev', split_axis=0, concat_axis=0, tiled=True)  50.1 us
    all_to_all x5, starting transfers between devices, exchange(): return lax.all_to_all(v, 'dev', split_axis=0, concat_axis=0, tiled=True)  34.5 us
    ppermute x8, waiting for transfers between devices, down(): return lax.ppermute(v, 'grp', down_pairs)  26.1 us
    ppermute x8, starting transfers between devices, down(): return lax.ppermute(v, 'grp', down_pairs)  25.6 us
    ppermute x8, waiting for transfers between devices, up(): return lax.ppermute(v, 'grp', up_pairs)  18.2 us
    pallas_call x3, Pallas kernels, score(): pl.pallas_call(functools.partial(score_kernel, per_dst=per_dst, carried=c...  13.3 us
    pallas_call x3, Pallas kernels, dispatch(): pl.pallas_call(functools.partial(dispatch_kernel, parts=[len(blocks) for...  7.13 us
    pallas_call x1, Pallas kernels, weight_gradient(): pl.pallas_call(functools.partial(weight_kernel, per_dst=per_dst), grid=(d...  6.5 us
  transfers between devices with their start and end apart: 21, of which 14 were waited for; matrix products, arithmetic and copies ran while one was open for 0% of the time, Pallas kernels for 11%

profile of v3, /device:TPU:2, one launch (start us, length us, event | category | flops | bytes accessed | tf_op | source)
XLA Modules:
  0.0 196.2 jit_solution(14692747509963608702)
XLA Ops:
  2.4 5.9 %collective-permute-start.3 = (bf16[144,1024]{1,0:T(8,128)(2,1)}, bf16[144,1024]{1,0:T(8,128)(2,1)S(1)}, u32[]{:S(2)}, u32[]{:S(2)}) collective-permute-start(bf16[144,1024]{1,0:T(8,128)(2,1)} %prepare.1.refs_0_), channel_id=1, source_target_pairs={{0,224},{32,0},{64,32},{96,64},{128,96},{160,128},{192,160},{224,1... | collective-permute-start | bytes 884744 | tf_op jit(solution)/shard_map/ppermute | solution.py:448
  10.9 7.6 %all-to-all-start = ((bf16[32,72,128]{2,1,0:T(8,128)(2,1)}), bf16[32,72,128]{2,1,0:T(8,128)(2,1)S(1)}, u32[]{:S(2)}, u32[]{:S(2)}) async-start(bf16[32,72,128]{2,1,0:T(8,128)(2,1)} %get-tuple-element.38), calls=%async_computation | async-start | bytes 1179648 | tf_op jit(solution)/shard_map/all_to_all | solution.py:451
  18.5 3.3 %collective-permute-start.4 = (bf16[144,1024]{1,0:T(8,128)(2,1)S(1)}, bf16[144,1024]{1,0:T(8,128)(2,1)S(1)}, u32[]{:S(2)}, u32[]{:S(2)}) collective-permute-start(bf16[144,1024]{1,0:T(8,128)(2,1)S(1)} %collective-permute-done.3.refs_1_), channel_id=1, source_target_pairs={{0,224},{32,0},{64,32},{96,64},{128,96},{160,128},{192,160},{224,1... | collective-permute-start | bytes 884744 | tf_op jit(solution)/shard_map/ppermute | solution.py:448
  21.8 6.6 %collective-permute-done.4.refs_3_ = bf16[144,1024]{1,0:T(8,128)(2,1)S(1)} collective-permute-done((bf16[144,1024]{1,0:T(8,128)(2,1)S(1)}, bf16[144,1024]{1,0:T(8,128)(2,1)S(1)}, u32[]{:S(2)}, u32[]{:S(2)}) %collective-permute-start.4) | collective-permute-done | bytes 294944 | tf_op jit(solution)/shard_map/ppermute | solution.py:448
  28.4 3.4 %collective-permute-done.1.refs_2_ = bf16[144,1024]{1,0:T(8,128)(2,1)S(1)} collective-permute-done((bf16[144,1024]{1,0:T(8,128)(2,1)S(1)}, bf16[144,1024]{1,0:T(8,128)(2,1)S(1)}, u32[]{:S(2)}, u32[]{:S(2)}) %collective-permute-start.1) | collective-permute-done | bytes 294944 | tf_op jit(solution)/shard_map/ppermute | solution.py:445
  31.8 3.1 %dispatch.4 = (bf16[32,264,128]{2,1,0:T(8,128)(2,1)}, bf16[4,256,128]{2,1,0:T(8,128)(2,1)S(1)}) custom-call(s32[1]{0:T(128)} %bitcast.grp_ref, bf16[144,1024]{1,0:T(8,128)(2,1)S(1)} %collective-permute-done.refs_0_, bf16[144,1024]{1,0:T(8,128)(2,1)S(1)} %collective-permute-done.3.refs_1_, bf16[144,1024]{1,0:T(8,128)(2,1)S(1)} %collective-permute-done.1.refs_2_, ...), custom_call_target="tpu_custom_call" | custom-call | tf_op jit(solution)/shard_map/dispatch/pallas_call | solution.py:151
  35.5 7.4 %all-to-all-start.1 = ((bf16[32,264,128]{2,1,0:T(8,128)(2,1)}), bf16[32,264,128]{2,1,0:T(8,128)(2,1)}, u32[]{:S(2)}, u32[]{:S(2)}) async-start(bf16[32,264,128]{2,1,0:T(8,128)(2,1)} %get-tuple-element.39), calls=%async_computation.1 | async-start | bytes 4325376 | tf_op jit(solution)/shard_map/all_to_all | solution.py:451
  45.1 7.0 %collective-permute-done.5.refs_1_ = bf16[144,1024]{1,0:T(8,128)(2,1)S(1)} collective-permute-done((bf16[144,1024]{1,0:T(8,128)(2,1)S(1)}, bf16[144,1024]{1,0:T(8,128)(2,1)S(1)}, u32[]{:S(2)}, u32[]{:S(2)}) %collective-permute-start.5) | collective-permute-done | bytes 294944 | tf_op jit(solution)/shard_map/ppermute | solution.py:448
  54.4 5.6 %collective-permute-done.6.refs_2_ = bf16[64,1024]{1,0:T(8,128)(2,1)S(1)} collective-permute-done((bf16[64,1024]{1,0:T(8,128)(2,1)S(1)}, bf16[64,1024]{1,0:T(8,128)(2,1)S(1)}, u32[]{:S(2)}, u32[]{:S(2)}) %collective-permute-start.6) | collective-permute-done | bytes 131104 | tf_op jit(solution)/shard_map/ppermute | solution.py:445
  60.0 2.5 %dispatch.3 = (bf16[32,200,128]{2,1,0:T(8,128)(2,1)}, bf16[3,256,128]{2,1,0:T(8,128)(2,1)S(1)}) custom-call(s32[1]{0:T(128)} %bitcast.grp_ref, bf16[144,1024]{1,0:T(8,128)(2,1)S(1)} %collective-permute-done.2.refs_0_, bf16[144,1024]{1,0:T(8,128)(2,1)S(1)} %collective-permute-done.5.refs_1_, bf16[64,1024]{1,0:T(8,128)(2,1)S(1)} %collective-permute-done.6.refs_2_, ...), custom_call_target="tpu_custom_call" | custom-call | tf_op jit(solution)/shard_map/dispatch/pallas_call | solution.py:151
  63.3 8.4 %all-to-all-done.1.x_ref.refs_2_ = bf16[32,264,128]{2,1,0:T(8,128)(2,1)} async-done(((bf16[32,264,128]{2,1,0:T(8,128)(2,1)}), bf16[32,264,128]{2,1,0:T(8,128)(2,1)}, u32[]{:S(2)}, u32[]{:S(2)}) %all-to-all-start.1) | async-done | bytes 2162720 | tf_op jit(solution)/shard_map/all_to_all | solution.py:451
  71.7 6.6 %all-to-all-start.2 = ((bf16[32,200,128]{2,1,0:T(8,128)(2,1)}), bf16[32,200,128]{2,1,0:T(8,128)(2,1)}, u32[]{:S(2)}, u32[]{:S(2)}) async-start(bf16[32,200,128]{2,1,0:T(8,128)(2,1)} %get-tuple-element.46), calls=%async_computation.2 | async-start | bytes 3276800 | tf_op jit(solution)/shard_map/all_to_all | solution.py:451
  78.4 2.1 %score.3 = (bf16[32,72,128]{2,1,0:T(8,128)(2,1)S(1)}, bf16[256,128]{1,0:T(8,128)(2,1)S(1)}) custom-call(s32[4]{0:T(128)S(1)} %copy-done.6, bf16[32,72,128]{2,1,0:T(8,128)(2,1)S(1)} %all-to-all-done.x_ref.refs_0_, bf16[512,1024]{1,0:T(8,128)(2,1)S(1)} %copy-done.5), custom_call_target="tpu_custom_call" | custom-call | flops 536870912 | bytes 2228224 | tf_op jit(solution)/shard_map/score/pallas_call | solution.py:247
  82.0 5.9 %score.4 = (bf16[32,200,128]{2,1,0:T(8,128)(2,1)}, bf16[32,136,128]{2,1,0:T(8,128)(2,1)}, bf16[1024,128]{1,0:T(8,128)(2,1)}) custom-call(s32[4]{0:T(128)} %count_ref.5, bf16[32,264,128]{2,1,0:T(8,128)(2,1)} %all-to-all-done.1.x_ref.refs_2_, bf16[512,1024]{1,0:T(8,128)(2,1)} %w_ref.5, bf16[32,72,128]{2,1,0:T(8,128)(2,1)} %copy-done.7), custom_call_target="tpu_custom_call" | custom-call | flops 2147483648 | bytes 5767168 | tf_op jit(solution)/shard_map/score/pallas_call | solution.py:247
  87.8 13.4 %all-to-all-done.2.x_ref.refs_4_ = bf16[32,200,128]{2,1,0:T(8,128)(2,1)} async-done(((bf16[32,200,128]{2,1,0:T(8,128)(2,1)}), bf16[32,200,128]{2,1,0:T(8,128)(2,1)}, u32[]{:S(2)}, u32[]{:S(2)}) %all-to-all-start.2) | async-done | bytes 1638432 | tf_op jit(solution)/shard_map/all_to_all | solution.py:451
  101.3 5.3 %score.5 = (bf16[32,328,128]{2,1,0:T(8,128)(2,1)}, bf16[768,128]{1,0:T(8,128)(2,1)}) custom-call(s32[4]{0:T(128)} %count_ref.5, bf16[32,200,128]{2,1,0:T(8,128)(2,1)} %all-to-all-done.2.x_ref.refs_4_, bf16[512,1024]{1,0:T(8,128)(2,1)} %w_ref.5, bf16[32,136,128]{2,1,0:T(8,128)(2,1)} %get-tuple-element.47.refs_0_), custom_call_target="tpu_custom_call" | custom-call | flops 1610612736 | bytes 4587520 | tf_op jit(solution)/shard_map/score/pallas_call | solution.py:247
  106.6 6.5 %all-to-all-start.3 = ((bf16[32,328,128]{2,1,0:T(8,128)(2,1)}), bf16[32,328,128]{2,1,0:T(8,128)(2,1)}, u32[]{:S(2)}, u32[]{:S(2)}) async-start(bf16[32,328,128]{2,1,0:T(8,128)(2,1)} %get-tuple-element.48), calls=%async_computation.3 | async-start | bytes 5373952 | tf_op jit(solution)/shard_map/all_to_all | solution.py:451
  113.1 6.5 %weight_gradient.1 = f32[512,1024]{1,0:T(8,128)} custom-call(bf16[32,72,128]{2,1,0:T(8,128)(2,1)} %copy-done.3, bf16[256,128]{1,0:T(8,128)(2,1)} %copy-done.8, bf16[32,264,128]{2,1,0:T(8,128)(2,1)} %all-to-all-done.1.x_ref.refs_2_, bf16[1024,128]{1,0:T(8,128)(2,1)} %get-tuple-element.50.refs_3_, bf16[32,200,128]{2,1,0:T(8,128)(2,1)} %all-to-all-done.2.x_ref.refs_4_, ...), custom_call_target="tpu_custom_call" | custom-call | flops 2147483648 | bytes 8388608 | tf_op jit(solution)/shard_map/weight_gradient/pallas_call | solution.py:304
  119.6 28.2 %all-to-all-done.3.ret_ref = bf16[32,328,128]{2,1,0:T(8,128)(2,1)} async-done(((bf16[32,328,128]{2,1,0:T(8,128)(2,1)}), bf16[32,328,128]{2,1,0:T(8,128)(2,1)}, u32[]{:S(2)}, u32[]{:S(2)}) %all-to-all-start.3) | async-done | bytes 2687008 | tf_op jit(solution)/shard_map/all_to_all | solution.py:451
  147.8 3.4 %combine.2 = (bf16[128,1152]{1,0:T(8,128)(2,1)}, bf16[128,1152]{1,0:T(8,128)(2,1)}, bf16[128,1152]{1,0:T(8,128)(2,1)}, bf16[128,1152]{1,0:T(8,128)(2,1)}, bf16[6...) custom-call(bf16[32,328,128]{2,1,0:T(8,128)(2,1)} %all-to-all-done.3.ret_ref, bf16[4,256,128]{2,1,0:T(8,128)(2,1)} %copy-done.1, ...), custom_call_target="tpu_custom_call" | custom-call | tf_op jit(solution)/shard_map/combine/pallas_call | solution.py:368
  151.4 6.2 %all-to-all-start.4 = ((bf16[32,200,128]{2,1,0:T(8,128)(2,1)}), bf16[32,200,128]{2,1,0:T(8,128)(2,1)S(1)}, u32[]{:S(2)}, u32[]{:S(2)}) async-start(bf16[32,200,128]{2,1,0:T(8,128)(2,1)} %get-tuple-element.52), calls=%async_computation.4 | async-start | bytes 3276800 | tf_op jit(solution)/shard_map/all_to_all | solution.py:451
  157.7 3.2 %collective-permute-start.8 = (bf16[64,1152]{1,0:T(8,128)(2,1)S(1)}, bf16[64,1152]{1,0:T(8,128)(2,1)S(1)}, u32[]{:S(2)}, u32[]{:S(2)}) collective-permute-start(bf16[64,1152]{1,0:T(8,128)(2,1)S(1)} %copy-done.13), channel_id=1, source_target_pairs={{0,224},{32,0},{64,32},{96,64},{128,96},{160,128},{192,160},{224,1... | collective-permute-start | bytes 442376 | tf_op jit(solution)/shard_map/ppermute | solution.py:448
  161.0 3.3 %collective-permute-done.8 = bf16[64,1152]{1,0:T(8,128)(2,1)S(1)} collective-permute-done((bf16[64,1152]{1,0:T(8,128)(2,1)S(1)}, bf16[64,1152]{1,0:T(8,128)(2,1)S(1)}, u32[]{:S(2)}, u32[]{:S(2)}) %collective-permute-start.8) | collective-permute-done | bytes 147488 | tf_op jit(solution)/shard_map/ppermute | solution.py:448
  164.3 3.8 %collective-permute-start.9 = (bf16[128,1152]{1,0:T(8,128)(2,1)S(1)}, bf16[128,1152]{1,0:T(8,128)(2,1)S(1)}, u32[]{:S(2)}, u32[]{:S(2)}) collective-permute-start(bf16[128,1152]{1,0:T(8,128)(2,1)S(1)} %add_convert_fusion.3), channel_id=1, source_target_pairs={{0,224},{32,0},{64,32},{96,64},{128,96},{160,128},{192,160},{224,1... | collective-permute-start | bytes 884744 | tf_op jit(solution)/shard_map/ppermute | solution.py:448
  168.1 2.9 %collective-permute-done.12 = bf16[128,1152]{1,0:T(8,128)(2,1)S(1)} collective-permute-done((bf16[128,1152]{1,0:T(8,128)(2,1)S(1)}, bf16[128,1152]{1,0:T(8,128)(2,1)S(1)}, u32[]{:S(2)}, u32[]{:S(2)}) %collective-permute-start.12) | collective-permute-done | bytes 294944 | tf_op jit(solution)/shard_map/ppermute | solution.py:445
  171.1 2.7 %collective-permute-done.9 = bf16[128,1152]{1,0:T(8,128)(2,1)S(1)} collective-permute-done((bf16[128,1152]{1,0:T(8,128)(2,1)S(1)}, bf16[128,1152]{1,0:T(8,128)(2,1)S(1)}, u32[]{:S(2)}, u32[]{:S(2)}) %collective-permute-start.9) | collective-permute-done | bytes 294944 | tf_op jit(solution)/shard_map/ppermute | solution.py:448
  173.9 3.8 %collective-permute-start.10 = (bf16[128,1152]{1,0:T(8,128)(2,1)S(1)}, bf16[128,1152]{1,0:T(8,128)(2,1)S(1)}, u32[]{:S(2)}, u32[]{:S(2)}) collective-permute-start(bf16[128,1152]{1,0:T(8,128)(2,1)S(1)} %add_convert_fusion.2), channel_id=1, source_target_pairs={{0,224},{32,0},{64,32},{96,64},{128,96},{160,128},{192,160},{224,1... | collective-permute-start | bytes 884744 | tf_op jit(solution)/shard_map/ppermute | solution.py:448
  177.7 2.6 %collective-permute-done.13.refs_3_ = bf16[128,1152]{1,0:T(8,128)(2,1)S(1)} collective-permute-done((bf16[128,1152]{1,0:T(8,128)(2,1)S(1)}, bf16[128,1152]{1,0:T(8,128)(2,1)S(1)}, u32[]{:S(2)}, u32[]{:S(2)}) %collective-permute-start.13) | collective-permute-done | bytes 294944 | tf_op jit(solution)/shard_map/ppermute | solution.py:445
  180.2 2.3 %collective-permute-done.10.refs_2_ = bf16[128,1152]{1,0:T(8,128)(2,1)S(1)} collective-permute-done((bf16[128,1152]{1,0:T(8,128)(2,1)S(1)}, bf16[128,1152]{1,0:T(8,128)(2,1)S(1)}, u32[]{:S(2)}, u32[]{:S(2)}) %collective-permute-start.10) | collective-permute-done | bytes 294944 | tf_op jit(solution)/shard_map/ppermute | solution.py:448
  183.4 3.8 %collective-permute-start.14 = (bf16[128,1152]{1,0:T(8,128)(2,1)S(1)}, bf16[128,1152]{1,0:T(8,128)(2,1)S(1)}, u32[]{:S(2)}, u32[]{:S(2)}) collective-permute-start(bf16[128,1152]{1,0:T(8,128)(2,1)S(1)} %get-tuple-element.64), channel_id=1, source_target_pairs={{0,224},{32,0},{64,32},{96,64},{128,96},{160,128},{192,160},{224,1... | collective-permute-start | bytes 884744 | tf_op jit(solution)/shard_map/ppermute | solution.py:448
  187.2 4.2 %collective-permute-done.14.lower_ref = bf16[128,1152]{1,0:T(8,128)(2,1)S(1)} collective-permute-done((bf16[128,1152]{1,0:T(8,128)(2,1)S(1)}, bf16[128,1152]{1,0:T(8,128)(2,1)S(1)}, u32[]{:S(2)}, u32[]{:S(2)}) %collective-permute-start.14) | collective-permute-done | bytes 294944 | tf_op jit(solution)/shard_map/ppermute | solution.py:448
  191.4 3.7 %collective-permute-done.15.upper_ref = bf16[128,1152]{1,0:T(8,128)(2,1)S(1)} collective-permute-done((bf16[128,1152]{1,0:T(8,128)(2,1)S(1)}, bf16[128,1152]{1,0:T(8,128)(2,1)S(1)}, u32[]{:S(2)}, u32[]{:S(2)}) %collective-permute-start.15) | collective-permute-done | bytes 294944 | tf_op jit(solution)/shard_map/ppermute | solution.py:445
  (55 shorter events, 13.7 us)
Async XLA Ops:
  2.4 16.1 %collective-permute-start.3 = (bf16[144,1024]{1,0:T(8,128)(2,1)}, bf16[144,1024]{1,0:T(8,128)(2,1)S(1)}, u32[]{:S(2)}, u32[]{:S(2)}) collective-permute-start(bf16[144,1024]{1,0:T(8,128)(2,1)} %prepare.1.refs_0_), channel_id=1, source_target_pairs={{0,224},{32,0},{64,32},{96,64},{128,96},{160,128},{192,160},{224,1... | collective-permute-start | bytes 884744 | tf_op jit(solution)/shard_map/ppermute | solution.py:448
  8.3 13.5 %collective-permute-start = (bf16[144,1024]{1,0:T(8,128)(2,1)}, bf16[144,1024]{1,0:T(8,128)(2,1)S(1)}, u32[]{:S(2)}, u32[]{:S(2)}) collective-permute-start(bf16[144,1024]{1,0:T(8,128)(2,1)} %prepare.1.refs_0_), channel_id=1, source_target_pairs={{0,32},{32,64},{64,96},{96,128},{128,160},{160,192},{192,224},{224... | collective-permute-start | bytes 884744 | tf_op jit(solution)/shard_map/ppermute | solution.py:445
  8.3 1.0 copy-start
  10.9 24.7 %all-to-all-start = ((bf16[32,72,128]{2,1,0:T(8,128)(2,1)}), bf16[32,72,128]{2,1,0:T(8,128)(2,1)S(1)}, u32[]{:S(2)}, u32[]{:S(2)}) async-start(bf16[32,72,128]{2,1,0:T(8,128)(2,1)} %get-tuple-element.38), calls=%async_computation | async-start | bytes 1179648 | tf_op jit(solution)/shard_map/all_to_all | solution.py:451
  18.5 9.9 %collective-permute-start.4 = (bf16[144,1024]{1,0:T(8,128)(2,1)S(1)}, bf16[144,1024]{1,0:T(8,128)(2,1)S(1)}, u32[]{:S(2)}, u32[]{:S(2)}) collective-permute-start(bf16[144,1024]{1,0:T(8,128)(2,1)S(1)} %collective-permute-done.3.refs_1_), channel_id=1, source_target_pairs={{0,224},{32,0},{64,32},{96,64},{128,96},{160,128},{192,160},{224,1... | collective-permute-start | bytes 884744 | tf_op jit(solution)/shard_map/ppermute | solution.py:448
  21.8 10.0 %collective-permute-start.1 = (bf16[144,1024]{1,0:T(8,128)(2,1)S(1)}, bf16[144,1024]{1,0:T(8,128)(2,1)S(1)}, u32[]{:S(2)}, u32[]{:S(2)}) collective-permute-start(bf16[144,1024]{1,0:T(8,128)(2,1)S(1)} %collective-permute-done.refs_0_), channel_id=1, source_target_pairs={{0,32},{32,64},{64,96},{96,128},{128,160},{160,192},{192,224},{224... | collective-permute-start | bytes 884744 | tf_op jit(solution)/shard_map/ppermute | solution.py:445
  35.5 42.8 %copy-start.3 = (bf16[32,72,128]{2,1,0:T(8,128)(2,1)}, bf16[32,72,128]{2,1,0:T(8,128)(2,1)S(1)}, u32[]{:S(2)}) copy-start(bf16[32,72,128]{2,1,0:T(8,128)(2,1)S(1)} %all-to-all-done.x_ref.refs_0_) | copy-start | bytes 1769476
  35.5 36.1 %all-to-all-start.1 = ((bf16[32,264,128]{2,1,0:T(8,128)(2,1)}), bf16[32,264,128]{2,1,0:T(8,128)(2,1)}, u32[]{:S(2)}, u32[]{:S(2)}) async-start(bf16[32,264,128]{2,1,0:T(8,128)(2,1)} %get-tuple-element.39), calls=%async_computation.1 | async-start | bytes 4325376 | tf_op jit(solution)/shard_map/all_to_all | solution.py:451
  43.0 9.1 %collective-permute-start.5 = (bf16[144,1024]{1,0:T(8,128)(2,1)S(1)}, bf16[144,1024]{1,0:T(8,128)(2,1)S(1)}, u32[]{:S(2)}, u32[]{:S(2)}) collective-permute-start(bf16[144,1024]{1,0:T(8,128)(2,1)S(1)} %collective-permute-done.4.refs_3_), channel_id=1, source_target_pairs={{0,224},{32,0},{64,32},{96,64},{128,96},{160,128},{192,160},{224,1... | collective-permute-start | bytes 884744 | tf_op jit(solution)/shard_map/ppermute | solution.py:448
  43.4 10.4 %collective-permute-start.2 = (bf16[144,1024]{1,0:T(8,128)(2,1)S(1)}, bf16[144,1024]{1,0:T(8,128)(2,1)S(1)}, u32[]{:S(2)}, u32[]{:S(2)}) collective-permute-start(bf16[144,1024]{1,0:T(8,128)(2,1)S(1)} %collective-permute-done.1.refs_2_), channel_id=1, source_target_pairs={{0,32},{32,64},{64,96},{96,128},{128,160},{160,192},{192,224},{224... | collective-permute-start | bytes 884744 | tf_op jit(solution)/shard_map/ppermute | solution.py:445
  52.2 7.9 %collective-permute-start.7 = (bf16[80,1024]{1,0:T(8,128)(2,1)S(1)}, bf16[80,1024]{1,0:T(8,128)(2,1)S(1)}, u32[]{:S(2)}, u32[]{:S(2)}) collective-permute-start(bf16[80,1024]{1,0:T(8,128)(2,1)S(1)} %slice.9), channel_id=1, source_target_pairs={{0,224},{32,0},{64,32},{96,64},{128,96},{160,128},{192,160},{224,1... | collective-permute-start | bytes 491528 | tf_op jit(solution)/shard_map/ppermute | solution.py:448
  53.7 24.6 %copy-start.5 = (bf16[512,1024]{1,0:T(8,128)(2,1)S(1)}, bf16[512,1024]{1,0:T(8,128)(2,1)}, u32[]{:S(2)}) copy-start(bf16[512,1024]{1,0:T(8,128)(2,1)} %w_ref.5) | copy-start | bytes 3145732
  53.8 24.6 %copy-start.6 = (s32[4]{0:T(128)S(1)}, s32[4]{0:T(128)}, u32[]{:S(2)}) copy-start(s32[4]{0:T(128)} %count_ref.5) | copy-start | bytes 52
  53.8 6.3 %collective-permute-start.6 = (bf16[64,1024]{1,0:T(8,128)(2,1)S(1)}, bf16[64,1024]{1,0:T(8,128)(2,1)S(1)}, u32[]{:S(2)}, u32[]{:S(2)}) collective-permute-start(bf16[64,1024]{1,0:T(8,128)(2,1)S(1)} %slice.8), channel_id=1, source_target_pairs={{0,32},{32,64},{64,96},{96,128},{128,160},{160,192},{192,224},{224... | collective-permute-start | bytes 393224 | tf_op jit(solution)/shard_map/ppermute | solution.py:445
  71.7 29.6 %all-to-all-start.2 = ((bf16[32,200,128]{2,1,0:T(8,128)(2,1)}), bf16[32,200,128]{2,1,0:T(8,128)(2,1)}, u32[]{:S(2)}, u32[]{:S(2)}) async-start(bf16[32,200,128]{2,1,0:T(8,128)(2,1)} %get-tuple-element.46), calls=%async_computation.2 | async-start | bytes 3276800 | tf_op jit(solution)/shard_map/all_to_all | solution.py:451
  80.5 0.8 copy-start.7
  106.6 41.2 %all-to-all-start.3 = ((bf16[32,328,128]{2,1,0:T(8,128)(2,1)}), bf16[32,328,128]{2,1,0:T(8,128)(2,1)}, u32[]{:S(2)}, u32[]{:S(2)}) async-start(bf16[32,328,128]{2,1,0:T(8,128)(2,1)} %get-tuple-element.48), calls=%async_computation.3 | async-start | bytes 5373952 | tf_op jit(solution)/shard_map/all_to_all | solution.py:451
  151.2 6.4 %copy-start.13 = (bf16[64,1152]{1,0:T(8,128)(2,1)S(1)}, bf16[64,1152]{1,0:T(8,128)(2,1)}, u32[]{:S(2)}) copy-start(bf16[64,1152]{1,0:T(8,128)(2,1)} %get-tuple-element.59) | copy-start | bytes 442372
  151.3 9.6 %copy-start.12 = (bf16[128,1152]{1,0:T(8,128)(2,1)S(1)}, bf16[128,1152]{1,0:T(8,128)(2,1)}, u32[]{:S(2)}) copy-start(bf16[128,1152]{1,0:T(8,128)(2,1)} %get-tuple-element.61) | copy-start | bytes 884740
  151.3 13.0 %copy-start.11 = (bf16[128,1152]{1,0:T(8,128)(2,1)S(1)}, bf16[128,1152]{1,0:T(8,128)(2,1)}, u32[]{:S(2)}) copy-start(bf16[128,1152]{1,0:T(8,128)(2,1)} %get-tuple-element.58) | copy-start | bytes 884740
  151.3 19.7 %copy-start.10 = (bf16[128,1152]{1,0:T(8,128)(2,1)S(1)}, bf16[128,1152]{1,0:T(8,128)(2,1)}, u32[]{:S(2)}) copy-start(bf16[128,1152]{1,0:T(8,128)(2,1)} %get-tuple-element.60) | copy-start | bytes 884740
  151.3 22.5 %copy-start.9 = (bf16[128,1152]{1,0:T(8,128)(2,1)S(1)}, bf16[128,1152]{1,0:T(8,128)(2,1)}, u32[]{:S(2)}) copy-start(bf16[128,1152]{1,0:T(8,128)(2,1)} %get-tuple-element.57) | copy-start | bytes 884740
  151.3 9.5 %collective-permute-start.11 = (bf16[64,1152]{1,0:T(8,128)(2,1)}, bf16[64,1152]{1,0:T(8,128)(2,1)S(1)}, u32[]{:S(2)}, u32[]{:S(2)}) collective-permute-start(bf16[64,1152]{1,0:T(8,128)(2,1)} %get-tuple-element.62), channel_id=1, source_target_pairs={{0,32},{32,64},{64,96},{96,128},{128,160},{160,192},{192,224},{224... | collective-permute-start | bytes 442376 | tf_op jit(solution)/shard_map/ppermute | solution.py:445
  151.4 31.1 %all-to-all-start.4 = ((bf16[32,200,128]{2,1,0:T(8,128)(2,1)}), bf16[32,200,128]{2,1,0:T(8,128)(2,1)S(1)}, u32[]{:S(2)}, u32[]{:S(2)}) async-start(bf16[32,200,128]{2,1,0:T(8,128)(2,1)} %get-tuple-element.52), calls=%async_computation.4 | async-start | bytes 3276800 | tf_op jit(solution)/shard_map/all_to_all | solution.py:451
  157.6 24.9 %copy-start.2 = (bf16[4,256,128]{2,1,0:T(8,128)(2,1)S(1)}, bf16[4,256,128]{2,1,0:T(8,128)(2,1)}, u32[]{:S(2)}) copy-start(bf16[4,256,128]{2,1,0:T(8,128)(2,1)} %copy-done.1) | copy-start | bytes 786436
  157.7 6.6 %collective-permute-start.8 = (bf16[64,1152]{1,0:T(8,128)(2,1)S(1)}, bf16[64,1152]{1,0:T(8,128)(2,1)S(1)}, u32[]{:S(2)}, u32[]{:S(2)}) collective-permute-start(bf16[64,1152]{1,0:T(8,128)(2,1)S(1)} %copy-done.13), channel_id=1, source_target_pairs={{0,224},{32,0},{64,32},{96,64},{128,96},{160,128},{192,160},{224,1... | collective-permute-start | bytes 442376 | tf_op jit(solution)/shard_map/ppermute | solution.py:448
  160.9 10.1 %collective-permute-start.12 = (bf16[128,1152]{1,0:T(8,128)(2,1)S(1)}, bf16[128,1152]{1,0:T(8,128)(2,1)S(1)}, u32[]{:S(2)}, u32[]{:S(2)}) collective-permute-start(bf16[128,1152]{1,0:T(8,128)(2,1)S(1)} %add_convert_fusion.1), channel_id=1, source_target_pairs={{0,32},{32,64},{64,96},{96,128},{128,160},{160,192},{192,224},{224... | collective-permute-start | bytes 884744 | tf_op jit(solution)/shard_map/ppermute | solution.py:445
  164.3 9.5 %collective-permute-start.9 = (bf16[128,1152]{1,0:T(8,128)(2,1)S(1)}, bf16[128,1152]{1,0:T(8,128)(2,1)S(1)}, u32[]{:S(2)}, u32[]{:S(2)}) collective-permute-start(bf16[128,1152]{1,0:T(8,128)(2,1)S(1)} %add_convert_fusion.3), channel_id=1, source_target_pairs={{0,224},{32,0},{64,32},{96,64},{128,96},{160,128},{192,160},{224,1... | collective-permute-start | bytes 884744 | tf_op jit(solution)/shard_map/ppermute | solution.py:448
  171.0 9.2 %collective-permute-start.13 = (bf16[128,1152]{1,0:T(8,128)(2,1)S(1)}, bf16[128,1152]{1,0:T(8,128)(2,1)S(1)}, u32[]{:S(2)}, u32[]{:S(2)}) collective-permute-start(bf16[128,1152]{1,0:T(8,128)(2,1)S(1)} %add_convert_fusion), channel_id=1, source_target_pairs={{0,32},{32,64},{64,96},{96,128},{128,160},{160,192},{192,224},{224... | collective-permute-start | bytes 884744 | tf_op jit(solution)/shard_map/ppermute | solution.py:445
  173.9 8.6 %collective-permute-start.10 = (bf16[128,1152]{1,0:T(8,128)(2,1)S(1)}, bf16[128,1152]{1,0:T(8,128)(2,1)S(1)}, u32[]{:S(2)}, u32[]{:S(2)}) collective-permute-start(bf16[128,1152]{1,0:T(8,128)(2,1)S(1)} %add_convert_fusion.2), channel_id=1, source_target_pairs={{0,224},{32,0},{64,32},{96,64},{128,96},{160,128},{192,160},{224,1... | collective-permute-start | bytes 884744 | tf_op jit(solution)/shard_map/ppermute | solution.py:448
  183.4 8.0 %collective-permute-start.14 = (bf16[128,1152]{1,0:T(8,128)(2,1)S(1)}, bf16[128,1152]{1,0:T(8,128)(2,1)S(1)}, u32[]{:S(2)}, u32[]{:S(2)}) collective-permute-start(bf16[128,1152]{1,0:T(8,128)(2,1)S(1)} %get-tuple-element.64), channel_id=1, source_target_pairs={{0,224},{32,0},{64,32},{96,64},{128,96},{160,128},{192,160},{224,1... | collective-permute-start | bytes 884744 | tf_op jit(solution)/shard_map/ppermute | solution.py:448
  187.2 7.9 %collective-permute-start.15 = (bf16[128,1152]{1,0:T(8,128)(2,1)S(1)}, bf16[128,1152]{1,0:T(8,128)(2,1)S(1)}, u32[]{:S(2)}, u32[]{:S(2)}) collective-permute-start(bf16[128,1152]{1,0:T(8,128)(2,1)S(1)} %get-tuple-element.65), channel_id=1, source_target_pairs={{0,32},{32,64},{64,96},{96,128},{128,160},{160,192},{192,224},{224... | collective-permute-start | bytes 884744 | tf_op jit(solution)/shard_map/ppermute | solution.py:445
  (3 other events, 2.0 us)

commit v4 on v3

--- a/solution.py
+++ b/solution.py
@@ -147,7 +147,7 @@
     width = flat[0].shape[1]
     send = (dsts, (len(sources) * width // LANES + 1) * TILE, LANES)
     pick = (len(sources), dsts * TILE, queries)
-    steps = 2
+    steps = 1
     return pl.pallas_call(
         functools.partial(
             dispatch_kernel,

time: 197 us -> 196 us (level)
  no operation moved by 1% of the time
where the time goes in v4:
time: 196 us
  waiting for transfers between devices  94.7 us (48%)
  starting transfers between devices  62.7 us (32%)
  Pallas kernels  32.9 us (17%)
  local copies, waits for them, and re-layouts  3.88 us (2%)
    all_to_all x5, waiting for transfers between devices, exchange(): return lax.all_to_all(v, 'dev', split_axis=0, concat_axis=0, tiled=True)  50.4 us
    all_to_all x5, starting transfers between devices, exchange(): return lax.all_to_all(v, 'dev', split_axis=0, concat_axis=0, tiled=True)  34.5 us
    ppermute x8, waiting for transfers between devices, down(): return lax.ppermute(v, 'grp', down_pairs)  26.1 us
    ppermute x8, starting transfers between devices, down(): return lax.ppermute(v, 'grp', down_pairs)  25.6 us
    ppermute x8, waiting for transfers between devices, up(): return lax.ppermute(v, 'grp', up_pairs)  18.2 us
    pallas_call x3, Pallas kernels, score(): pl.pallas_call(functools.partial(score_kernel, per_dst=per_dst, carried=c...  13.3 us
    pallas_call x1, Pallas kernels, weight_gradient(): pl.pallas_call(functools.partial(weight_kernel, per_dst=per_dst), grid=(d...  6.5 us
    pallas_call x3, Pallas kernels, dispatch(): pl.pallas_call(functools.partial(dispatch_kernel, parts=[len(blocks) for...  6.2 us
  transfers between devices with their start and end apart: 21, of which 14 were waited for; matrix products, arithmetic and copies ran while one was open for 0% of the time, Pallas kernels for 11%

profile of v4, /device:TPU:2, one launch (start us, length us, event | category | flops | bytes accessed | tf_op | source)
XLA Modules:
  0.0 195.6 jit_solution(17636907235050437456)
XLA Ops:
  2.4 5.9 %collective-permute-start.3 = (bf16[144,1024]{1,0:T(8,128)(2,1)}, bf16[144,1024]{1,0:T(8,128)(2,1)S(1)}, u32[]{:S(2)}, u32[]{:S(2)}) collective-permute-start(bf16[144,1024]{1,0:T(8,128)(2,1)} %prepare.1.refs_0_), channel_id=1, source_target_pairs={{0,224},{32,0},{64,32},{96,64},{128,96},{160,128},{192,160},{224,1... | collective-permute-start | bytes 884744 | tf_op jit(solution)/shard_map/ppermute | solution.py:448
  10.6 7.6 %all-to-all-start = ((bf16[32,72,128]{2,1,0:T(8,128)(2,1)}), bf16[32,72,128]{2,1,0:T(8,128)(2,1)S(1)}, u32[]{:S(2)}, u32[]{:S(2)}) async-start(bf16[32,72,128]{2,1,0:T(8,128)(2,1)} %get-tuple-element.38), calls=%async_computation | async-start | bytes 1179648 | tf_op jit(solution)/shard_map/all_to_all | solution.py:451
  18.3 3.3 %collective-permute-start.4 = (bf16[144,1024]{1,0:T(8,128)(2,1)S(1)}, bf16[144,1024]{1,0:T(8,128)(2,1)S(1)}, u32[]{:S(2)}, u32[]{:S(2)}) collective-permute-start(bf16[144,1024]{1,0:T(8,128)(2,1)S(1)} %collective-permute-done.3.refs_1_), channel_id=1, source_target_pairs={{0,224},{32,0},{64,32},{96,64},{128,96},{160,128},{192,160},{224,1... | collective-permute-start | bytes 884744 | tf_op jit(solution)/shard_map/ppermute | solution.py:448
  21.6 6.6 %collective-permute-done.4.refs_3_ = bf16[144,1024]{1,0:T(8,128)(2,1)S(1)} collective-permute-done((bf16[144,1024]{1,0:T(8,128)(2,1)S(1)}, bf16[144,1024]{1,0:T(8,128)(2,1)S(1)}, u32[]{:S(2)}, u32[]{:S(2)}) %collective-permute-start.4) | collective-permute-done | bytes 294944 | tf_op jit(solution)/shard_map/ppermute | solution.py:448
  28.1 3.4 %collective-permute-done.1.refs_2_ = bf16[144,1024]{1,0:T(8,128)(2,1)S(1)} collective-permute-done((bf16[144,1024]{1,0:T(8,128)(2,1)S(1)}, bf16[144,1024]{1,0:T(8,128)(2,1)S(1)}, u32[]{:S(2)}, u32[]{:S(2)}) %collective-permute-start.1) | collective-permute-done | bytes 294944 | tf_op jit(solution)/shard_map/ppermute | solution.py:445
  31.6 2.7 %dispatch.4 = (bf16[32,264,128]{2,1,0:T(8,128)(2,1)}, bf16[4,256,128]{2,1,0:T(8,128)(2,1)S(1)}) custom-call(s32[1]{0:T(128)} %bitcast.grp_ref, bf16[144,1024]{1,0:T(8,128)(2,1)S(1)} %collective-permute-done.refs_0_, bf16[144,1024]{1,0:T(8,128)(2,1)S(1)} %collective-permute-done.3.refs_1_, bf16[144,1024]{1,0:T(8,128)(2,1)S(1)} %collective-permute-done.1.refs_2_, ...), custom_call_target="tpu_custom_call" | custom-call | tf_op jit(solution)/shard_map/dispatch/pallas_call | solution.py:151
  34.9 7.4 %all-to-all-start.1 = ((bf16[32,264,128]{2,1,0:T(8,128)(2,1)}), bf16[32,264,128]{2,1,0:T(8,128)(2,1)}, u32[]{:S(2)}, u32[]{:S(2)}) async-start(bf16[32,264,128]{2,1,0:T(8,128)(2,1)} %get-tuple-element.39), calls=%async_computation.1 | async-start | bytes 4325376 | tf_op jit(solution)/shard_map/all_to_all | solution.py:451
  44.5 7.0 %collective-permute-done.5.refs_1_ = bf16[144,1024]{1,0:T(8,128)(2,1)S(1)} collective-permute-done((bf16[144,1024]{1,0:T(8,128)(2,1)S(1)}, bf16[144,1024]{1,0:T(8,128)(2,1)S(1)}, u32[]{:S(2)}, u32[]{:S(2)}) %collective-permute-start.5) | collective-permute-done | bytes 294944 | tf_op jit(solution)/shard_map/ppermute | solution.py:448
  53.8 5.6 %collective-permute-done.6.refs_2_ = bf16[64,1024]{1,0:T(8,128)(2,1)S(1)} collective-permute-done((bf16[64,1024]{1,0:T(8,128)(2,1)S(1)}, bf16[64,1024]{1,0:T(8,128)(2,1)S(1)}, u32[]{:S(2)}, u32[]{:S(2)}) %collective-permute-start.6) | collective-permute-done | bytes 131104 | tf_op jit(solution)/shard_map/ppermute | solution.py:445
  59.4 2.2 %dispatch.3 = (bf16[32,200,128]{2,1,0:T(8,128)(2,1)}, bf16[3,256,128]{2,1,0:T(8,128)(2,1)S(1)}) custom-call(s32[1]{0:T(128)} %bitcast.grp_ref, bf16[144,1024]{1,0:T(8,128)(2,1)S(1)} %collective-permute-done.2.refs_0_, bf16[144,1024]{1,0:T(8,128)(2,1)S(1)} %collective-permute-done.5.refs_1_, bf16[64,1024]{1,0:T(8,128)(2,1)S(1)} %collective-permute-done.6.refs_2_, ...), custom_call_target="tpu_custom_call" | custom-call | tf_op jit(solution)/shard_map/dispatch/pallas_call | solution.py:151
  62.3 8.8 %all-to-all-done.1.x_ref.refs_2_ = bf16[32,264,128]{2,1,0:T(8,128)(2,1)} async-done(((bf16[32,264,128]{2,1,0:T(8,128)(2,1)}), bf16[32,264,128]{2,1,0:T(8,128)(2,1)}, u32[]{:S(2)}, u32[]{:S(2)}) %all-to-all-start.1) | async-done | bytes 2162720 | tf_op jit(solution)/shard_map/all_to_all | solution.py:451
  71.1 6.6 %all-to-all-start.2 = ((bf16[32,200,128]{2,1,0:T(8,128)(2,1)}), bf16[32,200,128]{2,1,0:T(8,128)(2,1)}, u32[]{:S(2)}, u32[]{:S(2)}) async-start(bf16[32,200,128]{2,1,0:T(8,128)(2,1)} %get-tuple-element.46), calls=%async_computation.2 | async-start | bytes 3276800 | tf_op jit(solution)/shard_map/all_to_all | solution.py:451
  77.8 2.2 %score.3 = (bf16[32,72,128]{2,1,0:T(8,128)(2,1)S(1)}, bf16[256,128]{1,0:T(8,128)(2,1)S(1)}) custom-call(s32[4]{0:T(128)S(1)} %copy-done.6, bf16[32,72,128]{2,1,0:T(8,128)(2,1)S(1)} %all-to-all-done.x_ref.refs_0_, bf16[512,1024]{1,0:T(8,128)(2,1)S(1)} %copy-done.5), custom_call_target="tpu_custom_call" | custom-call | flops 536870912 | bytes 2228224 | tf_op jit(solution)/shard_map/score/pallas_call | solution.py:247
  81.4 5.9 %score.4 = (bf16[32,200,128]{2,1,0:T(8,128)(2,1)}, bf16[32,136,128]{2,1,0:T(8,128)(2,1)}, bf16[1024,128]{1,0:T(8,128)(2,1)}) custom-call(s32[4]{0:T(128)} %count_ref.5, bf16[32,264,128]{2,1,0:T(8,128)(2,1)} %all-to-all-done.1.x_ref.refs_2_, bf16[512,1024]{1,0:T(8,128)(2,1)} %w_ref.5, bf16[32,72,128]{2,1,0:T(8,128)(2,1)} %copy-done.7), custom_call_target="tpu_custom_call" | custom-call | flops 2147483648 | bytes 5767168 | tf_op jit(solution)/shard_map/score/pallas_call | solution.py:247
  87.2 13.4 %all-to-all-done.2.x_ref.refs_4_ = bf16[32,200,128]{2,1,0:T(8,128)(2,1)} async-done(((bf16[32,200,128]{2,1,0:T(8,128)(2,1)}), bf16[32,200,128]{2,1,0:T(8,128)(2,1)}, u32[]{:S(2)}, u32[]{:S(2)}) %all-to-all-start.2) | async-done | bytes 1638432 | tf_op jit(solution)/shard_map/all_to_all | solution.py:451
  100.6 5.3 %score.5 = (bf16[32,328,128]{2,1,0:T(8,128)(2,1)}, bf16[768,128]{1,0:T(8,128)(2,1)}) custom-call(s32[4]{0:T(128)} %count_ref.5, bf16[32,200,128]{2,1,0:T(8,128)(2,1)} %all-to-all-done.2.x_ref.refs_4_, bf16[512,1024]{1,0:T(8,128)(2,1)} %w_ref.5, bf16[32,136,128]{2,1,0:T(8,128)(2,1)} %get-tuple-element.47.refs_0_), custom_call_target="tpu_custom_call" | custom-call | flops 1610612736 | bytes 4587520 | tf_op jit(solution)/shard_map/score/pallas_call | solution.py:247
  105.9 6.5 %all-to-all-start.3 = ((bf16[32,328,128]{2,1,0:T(8,128)(2,1)}), bf16[32,328,128]{2,1,0:T(8,128)(2,1)}, u32[]{:S(2)}, u32[]{:S(2)}) async-start(bf16[32,328,128]{2,1,0:T(8,128)(2,1)} %get-tuple-element.48), calls=%async_computation.3 | async-start | bytes 5373952 | tf_op jit(solution)/shard_map/all_to_all | solution.py:451
  112.5 6.5 %weight_gradient.1 = f32[512,1024]{1,0:T(8,128)} custom-call(bf16[32,72,128]{2,1,0:T(8,128)(2,1)} %copy-done.3, bf16[256,128]{1,0:T(8,128)(2,1)} %copy-done.8, bf16[32,264,128]{2,1,0:T(8,128)(2,1)} %all-to-all-done.1.x_ref.refs_2_, bf16[1024,128]{1,0:T(8,128)(2,1)} %get-tuple-element.50.refs_3_, bf16[32,200,128]{2,1,0:T(8,128)(2,1)} %all-to-all-done.2.x_ref.refs_4_, ...), custom_call_target="tpu_custom_call" | custom-call | flops 2147483648 | bytes 8388608 | tf_op jit(solution)/shard_map/weight_gradient/pallas_call | solution.py:304
  119.0 28.2 %all-to-all-done.3.ret_ref = bf16[32,328,128]{2,1,0:T(8,128)(2,1)} async-done(((bf16[32,328,128]{2,1,0:T(8,128)(2,1)}), bf16[32,328,128]{2,1,0:T(8,128)(2,1)}, u32[]{:S(2)}, u32[]{:S(2)}) %all-to-all-start.3) | async-done | bytes 2687008 | tf_op jit(solution)/shard_map/all_to_all | solution.py:451
  147.2 3.4 %combine.2 = (bf16[128,1152]{1,0:T(8,128)(2,1)}, bf16[128,1152]{1,0:T(8,128)(2,1)}, bf16[128,1152]{1,0:T(8,128)(2,1)}, bf16[128,1152]{1,0:T(8,128)(2,1)}, bf16[6...) custom-call(bf16[32,328,128]{2,1,0:T(8,128)(2,1)} %all-to-all-done.3.ret_ref, bf16[4,256,128]{2,1,0:T(8,128)(2,1)} %copy-done.1, ...), custom_call_target="tpu_custom_call" | custom-call | tf_op jit(solution)/shard_map/combine/pallas_call | solution.py:368
  150.8 6.2 %all-to-all-start.4 = ((bf16[32,200,128]{2,1,0:T(8,128)(2,1)}), bf16[32,200,128]{2,1,0:T(8,128)(2,1)S(1)}, u32[]{:S(2)}, u32[]{:S(2)}) async-start(bf16[32,200,128]{2,1,0:T(8,128)(2,1)} %get-tuple-element.52), calls=%async_computation.4 | async-start | bytes 3276800 | tf_op jit(solution)/shard_map/all_to_all | solution.py:451
  157.1 3.2 %collective-permute-start.8 = (bf16[64,1152]{1,0:T(8,128)(2,1)S(1)}, bf16[64,1152]{1,0:T(8,128)(2,1)S(1)}, u32[]{:S(2)}, u32[]{:S(2)}) collective-permute-start(bf16[64,1152]{1,0:T(8,128)(2,1)S(1)} %copy-done.13), channel_id=1, source_target_pairs={{0,224},{32,0},{64,32},{96,64},{128,96},{160,128},{192,160},{224,1... | collective-permute-start | bytes 442376 | tf_op jit(solution)/shard_map/ppermute | solution.py:448
  160.4 3.3 %collective-permute-done.8 = bf16[64,1152]{1,0:T(8,128)(2,1)S(1)} collective-permute-done((bf16[64,1152]{1,0:T(8,128)(2,1)S(1)}, bf16[64,1152]{1,0:T(8,128)(2,1)S(1)}, u32[]{:S(2)}, u32[]{:S(2)}) %collective-permute-start.8) | collective-permute-done | bytes 147488 | tf_op jit(solution)/shard_map/ppermute | solution.py:448
  163.7 3.8 %collective-permute-start.9 = (bf16[128,1152]{1,0:T(8,128)(2,1)S(1)}, bf16[128,1152]{1,0:T(8,128)(2,1)S(1)}, u32[]{:S(2)}, u32[]{:S(2)}) collective-permute-start(bf16[128,1152]{1,0:T(8,128)(2,1)S(1)} %add_convert_fusion.3), channel_id=1, source_target_pairs={{0,224},{32,0},{64,32},{96,64},{128,96},{160,128},{192,160},{224,1... | collective-permute-start | bytes 884744 | tf_op jit(solution)/shard_map/ppermute | solution.py:448
  167.5 2.9 %collective-permute-done.12 = bf16[128,1152]{1,0:T(8,128)(2,1)S(1)} collective-permute-done((bf16[128,1152]{1,0:T(8,128)(2,1)S(1)}, bf16[128,1152]{1,0:T(8,128)(2,1)S(1)}, u32[]{:S(2)}, u32[]{:S(2)}) %collective-permute-start.12) | collective-permute-done | bytes 294944 | tf_op jit(solution)/shard_map/ppermute | solution.py:445
  170.5 2.7 %collective-permute-done.9 = bf16[128,1152]{1,0:T(8,128)(2,1)S(1)} collective-permute-done((bf16[128,1152]{1,0:T(8,128)(2,1)S(1)}, bf16[128,1152]{1,0:T(8,128)(2,1)S(1)}, u32[]{:S(2)}, u32[]{:S(2)}) %collective-permute-start.9) | collective-permute-done | bytes 294944 | tf_op jit(solution)/shard_map/ppermute | solution.py:448
  173.3 3.8 %collective-permute-start.10 = (bf16[128,1152]{1,0:T(8,128)(2,1)S(1)}, bf16[128,1152]{1,0:T(8,128)(2,1)S(1)}, u32[]{:S(2)}, u32[]{:S(2)}) collective-permute-start(bf16[128,1152]{1,0:T(8,128)(2,1)S(1)} %add_convert_fusion.2), channel_id=1, source_target_pairs={{0,224},{32,0},{64,32},{96,64},{128,96},{160,128},{192,160},{224,1... | collective-permute-start | bytes 884744 | tf_op jit(solution)/shard_map/ppermute | solution.py:448
  177.1 2.6 %collective-permute-done.13.refs_3_ = bf16[128,1152]{1,0:T(8,128)(2,1)S(1)} collective-permute-done((bf16[128,1152]{1,0:T(8,128)(2,1)S(1)}, bf16[128,1152]{1,0:T(8,128)(2,1)S(1)}, u32[]{:S(2)}, u32[]{:S(2)}) %collective-permute-start.13) | collective-permute-done | bytes 294944 | tf_op jit(solution)/shard_map/ppermute | solution.py:445
  179.6 2.3 %collective-permute-done.10.refs_2_ = bf16[128,1152]{1,0:T(8,128)(2,1)S(1)} collective-permute-done((bf16[128,1152]{1,0:T(8,128)(2,1)S(1)}, bf16[128,1152]{1,0:T(8,128)(2,1)S(1)}, u32[]{:S(2)}, u32[]{:S(2)}) %collective-permute-start.10) | collective-permute-done | bytes 294944 | tf_op jit(solution)/shard_map/ppermute | solution.py:448
  182.8 3.8 %collective-permute-start.14 = (bf16[128,1152]{1,0:T(8,128)(2,1)S(1)}, bf16[128,1152]{1,0:T(8,128)(2,1)S(1)}, u32[]{:S(2)}, u32[]{:S(2)}) collective-permute-start(bf16[128,1152]{1,0:T(8,128)(2,1)S(1)} %get-tuple-element.64), channel_id=1, source_target_pairs={{0,224},{32,0},{64,32},{96,64},{128,96},{160,128},{192,160},{224,1... | collective-permute-start | bytes 884744 | tf_op jit(solution)/shard_map/ppermute | solution.py:448
  186.6 4.2 %collective-permute-done.14.lower_ref = bf16[128,1152]{1,0:T(8,128)(2,1)S(1)} collective-permute-done((bf16[128,1152]{1,0:T(8,128)(2,1)S(1)}, bf16[128,1152]{1,0:T(8,128)(2,1)S(1)}, u32[]{:S(2)}, u32[]{:S(2)}) %collective-permute-start.14) | collective-permute-done | bytes 294944 | tf_op jit(solution)/shard_map/ppermute | solution.py:448
  190.8 3.7 %collective-permute-done.15.upper_ref = bf16[128,1152]{1,0:T(8,128)(2,1)S(1)} collective-permute-done((bf16[128,1152]{1,0:T(8,128)(2,1)S(1)}, bf16[128,1152]{1,0:T(8,128)(2,1)S(1)}, u32[]{:S(2)}, u32[]{:S(2)}) %collective-permute-start.15) | collective-permute-done | bytes 294944 | tf_op jit(solution)/shard_map/ppermute | solution.py:445
  (55 shorter events, 13.5 us)
Async XLA Ops:
  2.4 15.9 %collective-permute-start.3 = (bf16[144,1024]{1,0:T(8,128)(2,1)}, bf16[144,1024]{1,0:T(8,128)(2,1)S(1)}, u32[]{:S(2)}, u32[]{:S(2)}) collective-permute-start(bf16[144,1024]{1,0:T(8,128)(2,1)} %prepare.1.refs_0_), channel_id=1, source_target_pairs={{0,224},{32,0},{64,32},{96,64},{128,96},{160,128},{192,160},{224,1... | collective-permute-start | bytes 884744 | tf_op jit(solution)/shard_map/ppermute | solution.py:448
  8.3 13.3 %collective-permute-start = (bf16[144,1024]{1,0:T(8,128)(2,1)}, bf16[144,1024]{1,0:T(8,128)(2,1)S(1)}, u32[]{:S(2)}, u32[]{:S(2)}) collective-permute-start(bf16[144,1024]{1,0:T(8,128)(2,1)} %prepare.1.refs_0_), channel_id=1, source_target_pairs={{0,32},{32,64},{64,96},{96,128},{128,160},{160,192},{192,224},{224... | collective-permute-start | bytes 884744 | tf_op jit(solution)/shard_map/ppermute | solution.py:445
  8.3 1.0 copy-start
  10.6 24.3 %all-to-all-start = ((bf16[32,72,128]{2,1,0:T(8,128)(2,1)}), bf16[32,72,128]{2,1,0:T(8,128)(2,1)S(1)}, u32[]{:S(2)}, u32[]{:S(2)}) async-start(bf16[32,72,128]{2,1,0:T(8,128)(2,1)} %get-tuple-element.38), calls=%async_computation | async-start | bytes 1179648 | tf_op jit(solution)/shard_map/all_to_all | solution.py:451
  18.3 9.9 %collective-permute-start.4 = (bf16[144,1024]{1,0:T(8,128)(2,1)S(1)}, bf16[144,1024]{1,0:T(8,128)(2,1)S(1)}, u32[]{:S(2)}, u32[]{:S(2)}) collective-permute-start(bf16[144,1024]{1,0:T(8,128)(2,1)S(1)} %collective-permute-done.3.refs_1_), channel_id=1, source_target_pairs={{0,224},{32,0},{64,32},{96,64},{128,96},{160,128},{192,160},{224,1... | collective-permute-start | bytes 884744 | tf_op jit(solution)/shard_map/ppermute | solution.py:448
  21.6 10.0 %collective-permute-start.1 = (bf16[144,1024]{1,0:T(8,128)(2,1)S(1)}, bf16[144,1024]{1,0:T(8,128)(2,1)S(1)}, u32[]{:S(2)}, u32[]{:S(2)}) collective-permute-start(bf16[144,1024]{1,0:T(8,128)(2,1)S(1)} %collective-permute-done.refs_0_), channel_id=1, source_target_pairs={{0,32},{32,64},{64,96},{96,128},{128,160},{160,192},{192,224},{224... | collective-permute-start | bytes 884744 | tf_op jit(solution)/shard_map/ppermute | solution.py:445
  34.9 42.8 %copy-start.3 = (bf16[32,72,128]{2,1,0:T(8,128)(2,1)}, bf16[32,72,128]{2,1,0:T(8,128)(2,1)S(1)}, u32[]{:S(2)}) copy-start(bf16[32,72,128]{2,1,0:T(8,128)(2,1)S(1)} %all-to-all-done.x_ref.refs_0_) | copy-start | bytes 1769476
  34.9 36.1 %all-to-all-start.1 = ((bf16[32,264,128]{2,1,0:T(8,128)(2,1)}), bf16[32,264,128]{2,1,0:T(8,128)(2,1)}, u32[]{:S(2)}, u32[]{:S(2)}) async-start(bf16[32,264,128]{2,1,0:T(8,128)(2,1)} %get-tuple-element.39), calls=%async_computation.1 | async-start | bytes 4325376 | tf_op jit(solution)/shard_map/all_to_all | solution.py:451
  42.4 9.1 %collective-permute-start.5 = (bf16[144,1024]{1,0:T(8,128)(2,1)S(1)}, bf16[144,1024]{1,0:T(8,128)(2,1)S(1)}, u32[]{:S(2)}, u32[]{:S(2)}) collective-permute-start(bf16[144,1024]{1,0:T(8,128)(2,1)S(1)} %collective-permute-done.4.refs_3_), channel_id=1, source_target_pairs={{0,224},{32,0},{64,32},{96,64},{128,96},{160,128},{192,160},{224,1... | collective-permute-start | bytes 884744 | tf_op jit(solution)/shard_map/ppermute | solution.py:448
  42.7 10.4 %collective-permute-start.2 = (bf16[144,1024]{1,0:T(8,128)(2,1)S(1)}, bf16[144,1024]{1,0:T(8,128)(2,1)S(1)}, u32[]{:S(2)}, u32[]{:S(2)}) collective-permute-start(bf16[144,1024]{1,0:T(8,128)(2,1)S(1)} %collective-permute-done.1.refs_2_), channel_id=1, source_target_pairs={{0,32},{32,64},{64,96},{96,128},{128,160},{160,192},{192,224},{224... | collective-permute-start | bytes 884744 | tf_op jit(solution)/shard_map/ppermute | solution.py:445
  51.5 7.9 %collective-permute-start.7 = (bf16[80,1024]{1,0:T(8,128)(2,1)S(1)}, bf16[80,1024]{1,0:T(8,128)(2,1)S(1)}, u32[]{:S(2)}, u32[]{:S(2)}) collective-permute-start(bf16[80,1024]{1,0:T(8,128)(2,1)S(1)} %slice.9), channel_id=1, source_target_pairs={{0,224},{32,0},{64,32},{96,64},{128,96},{160,128},{192,160},{224,1... | collective-permute-start | bytes 491528 | tf_op jit(solution)/shard_map/ppermute | solution.py:448
  53.1 24.6 %copy-start.5 = (bf16[512,1024]{1,0:T(8,128)(2,1)S(1)}, bf16[512,1024]{1,0:T(8,128)(2,1)}, u32[]{:S(2)}) copy-start(bf16[512,1024]{1,0:T(8,128)(2,1)} %w_ref.5) | copy-start | bytes 3145732
  53.1 24.6 %copy-start.6 = (s32[4]{0:T(128)S(1)}, s32[4]{0:T(128)}, u32[]{:S(2)}) copy-start(s32[4]{0:T(128)} %count_ref.5) | copy-start | bytes 52
  53.2 6.3 %collective-permute-start.6 = (bf16[64,1024]{1,0:T(8,128)(2,1)S(1)}, bf16[64,1024]{1,0:T(8,128)(2,1)S(1)}, u32[]{:S(2)}, u32[]{:S(2)}) collective-permute-start(bf16[64,1024]{1,0:T(8,128)(2,1)S(1)} %slice.8), channel_id=1, source_target_pairs={{0,32},{32,64},{64,96},{96,128},{128,160},{160,192},{192,224},{224... | collective-permute-start | bytes 393224 | tf_op jit(solution)/shard_map/ppermute | solution.py:445
  71.1 29.6 %all-to-all-start.2 = ((bf16[32,200,128]{2,1,0:T(8,128)(2,1)}), bf16[32,200,128]{2,1,0:T(8,128)(2,1)}, u32[]{:S(2)}, u32[]{:S(2)}) async-start(bf16[32,200,128]{2,1,0:T(8,128)(2,1)} %get-tuple-element.46), calls=%async_computation.2 | async-start | bytes 3276800 | tf_op jit(solution)/shard_map/all_to_all | solution.py:451
  79.9 0.8 copy-start.7
  105.9 41.3 %all-to-all-start.3 = ((bf16[32,328,128]{2,1,0:T(8,128)(2,1)}), bf16[32,328,128]{2,1,0:T(8,128)(2,1)}, u32[]{:S(2)}, u32[]{:S(2)}) async-start(bf16[32,328,128]{2,1,0:T(8,128)(2,1)} %get-tuple-element.48), calls=%async_computation.3 | async-start | bytes 5373952 | tf_op jit(solution)/shard_map/all_to_all | solution.py:451
  150.6 6.4 %copy-start.13 = (bf16[64,1152]{1,0:T(8,128)(2,1)S(1)}, bf16[64,1152]{1,0:T(8,128)(2,1)}, u32[]{:S(2)}) copy-start(bf16[64,1152]{1,0:T(8,128)(2,1)} %get-tuple-element.59) | copy-start | bytes 442372
  150.7 9.6 %copy-start.12 = (bf16[128,1152]{1,0:T(8,128)(2,1)S(1)}, bf16[128,1152]{1,0:T(8,128)(2,1)}, u32[]{:S(2)}) copy-start(bf16[128,1152]{1,0:T(8,128)(2,1)} %get-tuple-element.61) | copy-start | bytes 884740
  150.7 13.0 %copy-start.11 = (bf16[128,1152]{1,0:T(8,128)(2,1)S(1)}, bf16[128,1152]{1,0:T(8,128)(2,1)}, u32[]{:S(2)}) copy-start(bf16[128,1152]{1,0:T(8,128)(2,1)} %get-tuple-element.58) | copy-start | bytes 884740
  150.7 19.7 %copy-start.10 = (bf16[128,1152]{1,0:T(8,128)(2,1)S(1)}, bf16[128,1152]{1,0:T(8,128)(2,1)}, u32[]{:S(2)}) copy-start(bf16[128,1152]{1,0:T(8,128)(2,1)} %get-tuple-element.60) | copy-start | bytes 884740
  150.7 22.5 %copy-start.9 = (bf16[128,1152]{1,0:T(8,128)(2,1)S(1)}, bf16[128,1152]{1,0:T(8,128)(2,1)}, u32[]{:S(2)}) copy-start(bf16[128,1152]{1,0:T(8,128)(2,1)} %get-tuple-element.57) | copy-start | bytes 884740
  150.7 9.5 %collective-permute-start.11 = (bf16[64,1152]{1,0:T(8,128)(2,1)}, bf16[64,1152]{1,0:T(8,128)(2,1)S(1)}, u32[]{:S(2)}, u32[]{:S(2)}) collective-permute-start(bf16[64,1152]{1,0:T(8,128)(2,1)} %get-tuple-element.62), channel_id=1, source_target_pairs={{0,32},{32,64},{64,96},{96,128},{128,160},{160,192},{192,224},{224... | collective-permute-start | bytes 442376 | tf_op jit(solution)/shard_map/ppermute | solution.py:445
  150.8 31.1 %all-to-all-start.4 = ((bf16[32,200,128]{2,1,0:T(8,128)(2,1)}), bf16[32,200,128]{2,1,0:T(8,128)(2,1)S(1)}, u32[]{:S(2)}, u32[]{:S(2)}) async-start(bf16[32,200,128]{2,1,0:T(8,128)(2,1)} %get-tuple-element.52), calls=%async_computation.4 | async-start | bytes 3276800 | tf_op jit(solution)/shard_map/all_to_all | solution.py:451
  157.0 24.9 %copy-start.2 = (bf16[4,256,128]{2,1,0:T(8,128)(2,1)S(1)}, bf16[4,256,128]{2,1,0:T(8,128)(2,1)}, u32[]{:S(2)}) copy-start(bf16[4,256,128]{2,1,0:T(8,128)(2,1)} %copy-done.1) | copy-start | bytes 786436
  157.1 6.6 %collective-permute-start.8 = (bf16[64,1152]{1,0:T(8,128)(2,1)S(1)}, bf16[64,1152]{1,0:T(8,128)(2,1)S(1)}, u32[]{:S(2)}, u32[]{:S(2)}) collective-permute-start(bf16[64,1152]{1,0:T(8,128)(2,1)S(1)} %copy-done.13), channel_id=1, source_target_pairs={{0,224},{32,0},{64,32},{96,64},{128,96},{160,128},{192,160},{224,1... | collective-permute-start | bytes 442376 | tf_op jit(solution)/shard_map/ppermute | solution.py:448
  160.3 10.1 %collective-permute-start.12 = (bf16[128,1152]{1,0:T(8,128)(2,1)S(1)}, bf16[128,1152]{1,0:T(8,128)(2,1)S(1)}, u32[]{:S(2)}, u32[]{:S(2)}) collective-permute-start(bf16[128,1152]{1,0:T(8,128)(2,1)S(1)} %add_convert_fusion.1), channel_id=1, source_target_pairs={{0,32},{32,64},{64,96},{96,128},{128,160},{160,192},{192,224},{224... | collective-permute-start | bytes 884744 | tf_op jit(solution)/shard_map/ppermute | solution.py:445
  163.7 9.5 %collective-permute-start.9 = (bf16[128,1152]{1,0:T(8,128)(2,1)S(1)}, bf16[128,1152]{1,0:T(8,128)(2,1)S(1)}, u32[]{:S(2)}, u32[]{:S(2)}) collective-permute-start(bf16[128,1152]{1,0:T(8,128)(2,1)S(1)} %add_convert_fusion.3), channel_id=1, source_target_pairs={{0,224},{32,0},{64,32},{96,64},{128,96},{160,128},{192,160},{224,1... | collective-permute-start | bytes 884744 | tf_op jit(solution)/shard_map/ppermute | solution.py:448
  170.4 9.2 %collective-permute-start.13 = (bf16[128,1152]{1,0:T(8,128)(2,1)S(1)}, bf16[128,1152]{1,0:T(8,128)(2,1)S(1)}, u32[]{:S(2)}, u32[]{:S(2)}) collective-permute-start(bf16[128,1152]{1,0:T(8,128)(2,1)S(1)} %add_convert_fusion), channel_id=1, source_target_pairs={{0,32},{32,64},{64,96},{96,128},{128,160},{160,192},{192,224},{224... | collective-permute-start | bytes 884744 | tf_op jit(solution)/shard_map/ppermute | solution.py:445
  173.3 8.6 %collective-permute-start.10 = (bf16[128,1152]{1,0:T(8,128)(2,1)S(1)}, bf16[128,1152]{1,0:T(8,128)(2,1)S(1)}, u32[]{:S(2)}, u32[]{:S(2)}) collective-permute-start(bf16[128,1152]{1,0:T(8,128)(2,1)S(1)} %add_convert_fusion.2), channel_id=1, source_target_pairs={{0,224},{32,0},{64,32},{96,64},{128,96},{160,128},{192,160},{224,1... | collective-permute-start | bytes 884744 | tf_op jit(solution)/shard_map/ppermute | solution.py:448
  182.8 8.0 %collective-permute-start.14 = (bf16[128,1152]{1,0:T(8,128)(2,1)S(1)}, bf16[128,1152]{1,0:T(8,128)(2,1)S(1)}, u32[]{:S(2)}, u32[]{:S(2)}) collective-permute-start(bf16[128,1152]{1,0:T(8,128)(2,1)S(1)} %get-tuple-element.64), channel_id=1, source_target_pairs={{0,224},{32,0},{64,32},{96,64},{128,96},{160,128},{192,160},{224,1... | collective-permute-start | bytes 884744 | tf_op jit(solution)/shard_map/ppermute | solution.py:448
  186.6 7.9 %collective-permute-start.15 = (bf16[128,1152]{1,0:T(8,128)(2,1)S(1)}, bf16[128,1152]{1,0:T(8,128)(2,1)S(1)}, u32[]{:S(2)}, u32[]{:S(2)}) collective-permute-start(bf16[128,1152]{1,0:T(8,128)(2,1)S(1)} %get-tuple-element.65), channel_id=1, source_target_pairs={{0,32},{32,64},{64,96},{96,128},{128,160},{160,192},{192,224},{224... | collective-permute-start | bytes 884744 | tf_op jit(solution)/shard_map/ppermute | solution.py:445
  (3 other events, 2.0 us)
